TPU v7x, 32 devices: a whole 2x2x4 slice. The times are simulated.
32 devices in a mesh: rows: 4 (over z), cols: 8 (over y, x, core).
Axes of the slice: x: 2, y: 2, z: 4, core: 2. Of those that a mesh axis runs over, the one named last changes fastest.
Arguments:
- model_dir: float32 [65536, 128], P('cols'), may hold values from -6 to 6
- sens_blocks: bfloat16 [4, 3072, 128, 128], P('rows', 'cols'), may hold values from -0.09375 to 0.09375
- blk_row: int32 [4, 3072], P('rows', 'cols'), may hold values from 0 to 31, as said below
- blk_col: int32 [4, 3072], P('rows', 'cols'), may hold values from 0 to 63, as said below
- blk_count: int32 [4, 8], P('rows', 'cols'), may hold values from 48 to 384, as said below
- send_order: int32 [8, 64], P('cols'), may hold values from 0 to 63, each once within a row
- neighbors: int32 [4, 65536], P(None, 'cols'), may hold values from 0 to 65535, as said below
- face_weight: float32 [4, 65536], P(None, 'cols'), may hold values from 0.05 to 0.5
Outputs:
- data_image: float32 [16384, 128], P('rows')
- normal_product: float32 [65536, 128], P('cols')
Inputs may be any that keep to these rules, and one draw needn't show every extreme that they name: Within one device's 384 slots the pairs (blk_row, blk_col) are all different. `blk_col`: paired with blk_row as stated there. The live slots of a device are its first blk_count slots; some device has all 384 live. `send_order`: each row is a permutation. `neighbors`: every neighbour lies within 64 of the cell's own number.
All inputs are finite; a program needn't handle non-finite values.
Results may differ from a plain program's by a relative error of at most 0.0029.
Values may be sent and summed in bfloat16 or wider, within the bound.
No kernel may reach another device: no remote copies, remote signals or barrier semaphores. Data moves between devices by JAX's collectives and lax.ppermute only.
A program may use at most 192 MiB of HBM per device.

v0:
```python
import math

import jax
import jax.numpy as jnp
import numpy as np
from jax import lax
from jax.experimental import pallas as pl
from jax.experimental.pallas import tpu as pltpu
from jax.sharding import PartitionSpec as P

BLK = 128
RB_DEV = 32
RIM = 64
STEP = 16
MIB = 1 << 20
SMALL = 16 * MIB
LARGE = 56 * MIB
ANY_SPEC = pl.BlockSpec(memory_space=pl.ANY)
VMEM_SPEC = pl.BlockSpec(memory_space=pltpu.VMEM)
SMEM_SPEC = pl.BlockSpec(memory_space=pltpu.SMEM)


def haar_matrix(order_n):
    matrix = np.ones((1, 1))
    while matrix.shape[0] < order_n:
        length = matrix.shape[0]
        upper = np.kron(matrix, np.array([[1.0, 1.0]]))
        lower = np.kron(np.eye(length), np.array([[1.0, -1.0]]))
        matrix = np.concatenate([upper, lower], axis=0) / math.sqrt(2.0)
    return matrix


def fetch(source, target, sems, pieces):
    each = source.shape[0] // pieces
    parts = [pl.ds(i * each, each) for i in range(pieces)]
    return [
        pltpu.make_async_copy(source.at[part], target.at[part], sems.at[i])
        for i, part in enumerate(parts)
    ]


def gather_pieces(sources, held_ref, me, sems):
    each = held_ref.shape[0] // len(sources)
    return [
        pltpu.make_async_copy(
            ref.at[pl.ds(first * each, each)],
            held_ref.at[pl.ds((me ^ offset) * each, each)],
            sems.at[offset],
        )
        for offset, (ref, first) in enumerate(sources)
    ]


def piece_stores(source, offset, even_refs, odd_ref, sems):
    each = odd_ref.shape[0] // (sems.shape[0] // 2)
    if offset % 2:
        target = odd_ref.at[pl.ds((offset // 2) * each, each)]
    else:
        target = even_refs[offset // 2]
    return pltpu.make_async_copy(source, target, sems.at[offset])


def start_all(copies):
    for copy in copies:
        copy.start()


def wait_all(copies):
    for copy in copies:
        copy.wait()


def analyze_body(me_ref, order_ref, model_ref, *refs):
    even_refs, (odd_ref, block_ref, coeff_ref, got, put) = refs[:-5], refs[-5:]
    width = model_ref.shape[2]
    per_peer = even_refs[0].shape[0]
    peers = put.shape[0]
    me = me_ref[0]
    loads = fetch(model_ref, block_ref, got, got.shape[0])
    start_all(loads)
    row = lax.broadcasted_iota(jnp.int32, (BLK, BLK), 0)
    col = lax.broadcasted_iota(jnp.int32, (BLK, BLK), 1)
    level = jnp.ones_like(row)
    scale = jnp.full((BLK, width), BLK**-0.5, jnp.float32)
    wide_row = lax.broadcasted_iota(jnp.int32, (BLK, width), 0)
    size = 2
    while size < BLK:
        level = jnp.where(row >= size, size, level)
        scale = jnp.where(wide_row >= size, (size / BLK) ** 0.5, scale)
        size *= 2
    span = BLK // level
    inside = col - (row - level) * span
    sign = jnp.where(inside * 2 < span, 1.0, -1.0)
    sign = jnp.where((inside >= 0) & (inside < span), sign, 0.0)
    sign = jnp.where(row == 0, 1.0, sign).astype(jnp.bfloat16)
    both_signs = jnp.concatenate([sign, sign], axis=1)
    wait_all(loads)
    stores = []
    for offset in [*range(1, peers, 2), *range(peers - 2, -1, -2)]:
        peer = (me ^ offset) * per_peer
        for q in range(per_peer):
            x = block_ref[order_ref[0, peer + q]]
            high = x.astype(jnp.bfloat16)
            low = (x - high.astype(jnp.float32)).astype(jnp.bfloat16)
            raw = jnp.dot(
                both_signs, jnp.concatenate([high, low], axis=0),
                preferred_element_type=jnp.float32,
            )
            coeff_ref[offset, q] = (raw * scale).astype(jnp.bfloat16)
        stores.append(piece_stores(coeff_ref.at[offset], offset, even_refs, odd_ref, put))
        stores[-1].start()
    wait_all(stores)


def piece_shapes(piece, peers, dtype):
    half = peers // 2
    return [jax.ShapeDtypeStruct(piece, dtype)] * half + [
        jax.ShapeDtypeStruct((half * piece[0], *piece[1:]), dtype)
    ]


def analyze(me, order, model_blocks, peers):
    blocks, _, width = model_blocks.shape
    piece = (blocks // peers, BLK, width)
    return pl.pallas_call(
        analyze_body,
        out_shape=piece_shapes(piece, peers, jnp.bfloat16),
        in_specs=[SMEM_SPEC, SMEM_SPEC, ANY_SPEC],
        out_specs=[ANY_SPEC] * (peers // 2 + 1),
        scratch_shapes=[
            pltpu.VMEM((blocks, BLK, width), jnp.float32),
            pltpu.VMEM((peers, *piece), jnp.bfloat16),
            pltpu.SemaphoreType.DMA((16,)),
            pltpu.SemaphoreType.DMA((peers,)),
        ],
        compiler_params=pltpu.CompilerParams(vmem_limit_bytes=LARGE),
        cost_estimate=pl.CostEstimate(
            flops=4 * blocks * BLK * BLK * width, bytes_accessed=6 * blocks * BLK * width,
            transcendentals=0,
        ),
        name="analyze",
    )(me, order, model_blocks)


def slot_loop(count, sens_ref, block_ref, sems, others, work):
    steps = sems.shape[0]
    each = sens_ref.shape[0] // steps

    def block_copy(step):
        part = pl.ds(step * each, each)
        return pltpu.make_async_copy(sens_ref.at[part], block_ref.at[part], sems.at[step])

    start_all(others)
    needed = (count + each - 1) // each

    @pl.loop(0, needed)
    def _(step):
        block_copy(step).start()

    wait_all(others)

    @pl.loop(0, needed)
    def _(step):
        block_copy(step).wait()
        for k in range(each):
            slot = step * each + k
            work(slot, block_ref[slot], slot < count)


def forward_body(me_ref, rows_ref, cols_ref, count_ref, sens_ref, *refs):
    peers = len(refs) - 9
    wave_refs, (even_ref, odd_ref) = refs[:peers], refs[peers + 1 : peers + 3]
    block_ref, held_ref, acc_ref, sems, got, put = refs[peers + 3 :]
    row_blocks = acc_ref.shape[0] - 1
    each = row_blocks // peers
    me = me_ref[0]
    acc_ref[...] = jnp.zeros_like(acc_ref)

    def work(slot, block, live):
        row = jnp.where(live, rows_ref[0, slot], row_blocks)
        acc_ref[row] += jnp.dot(
            block, held_ref[cols_ref[0, slot]], preferred_element_type=jnp.float32
        )

    waves = gather_pieces([(ref, 0) for ref in wave_refs], held_ref, me, got)
    slot_loop(count_ref[0, 0], sens_ref, block_ref, sems, waves, work)
    stores = []
    for offset in [*range(1, peers, 2), *range(0, peers, 2)]:
        target = odd_ref if offset % 2 else even_ref
        stores.append(
            pltpu.make_async_copy(
                acc_ref.at[pl.ds((me ^ offset) * each, each)],
                target.at[pl.ds((offset // 2) * each, each)],
                put.at[offset],
            )
        )
    start_all(stores)
    wait_all(stores)


def forward(me, rows, cols, count, sens, waves, after):
    slots = sens.shape[0]
    peers = len(waves)
    blocks, width = after[1], sens.shape[2]
    half = (RB_DEV // 2, BLK, width)
    return pl.pallas_call(
        forward_body,
        out_shape=[jax.ShapeDtypeStruct(half, jnp.float32)] * 2,
        in_specs=[SMEM_SPEC] * 4 + [ANY_SPEC] * (1 + peers + 1),
        out_specs=[ANY_SPEC] * 2,
        scratch_shapes=[
            pltpu.VMEM(sens.shape, sens.dtype),
            pltpu.VMEM((blocks, BLK, width), jnp.bfloat16),
            pltpu.VMEM((RB_DEV + 1, BLK, width), jnp.float32),
            pltpu.SemaphoreType.DMA((slots // STEP,)),
            pltpu.SemaphoreType.DMA((peers,)),
            pltpu.SemaphoreType.DMA((peers,)),
        ],
        compiler_params=pltpu.CompilerParams(vmem_limit_bytes=LARGE),
        cost_estimate=pl.CostEstimate(
            flops=2 * slots * BLK * BLK * width, bytes_accessed=2 * slots * BLK * BLK,
            transcendentals=0,
        ),
        name="forward",
    )(me, rows, cols, count, sens, *waves, after[0])


def adjoint_body(me_ref, rows_ref, cols_ref, count_ref, sens_ref, even_in_ref, odd_in_ref,
                 after_ref, *refs):
    even_refs, (odd_ref, image_ref) = refs[:-10], refs[-10:-8]
    block_ref, held_ref, acc_ref, half_ref, sems, got, put, whole = refs[-8:]
    peers = put.shape[0]
    col_blocks = acc_ref.shape[0] - 1
    each = col_blocks // peers
    me = me_ref[0]
    acc_ref[...] = jnp.zeros_like(acc_ref)

    def work(slot, block, live):
        col = jnp.where(live, cols_ref[0, slot], col_blocks)
        acc_ref[col] += lax.dot_general(
            block, held_ref[rows_ref[0, slot]], (((0,), (0,)), ((), ())),
            preferred_element_type=jnp.float32,
        )

    sources = [(odd_in_ref if o % 2 else even_in_ref, o // 2) for o in range(peers)]
    images = gather_pieces(sources, held_ref, me, got)
    slot_loop(count_ref[0, 0], sens_ref, block_ref, sems, images, work)
    stores = []
    for offset in [0, *range(1, peers, 2), *range(2, peers, 2)]:
        part = acc_ref[pl.ds((me ^ offset) * each, each)]
        half_ref[offset] = part.astype(half_ref.dtype)
        stores.append(piece_stores(half_ref.at[offset], offset, even_refs, odd_ref, put))
        stores[-1].start()
    stores.extend(fetch(held_ref, image_ref, whole, whole.shape[0]))
    start_all(stores[peers:])
    wait_all(stores)


def adjoint(me, rows, cols, count, sens, even, odd, after, blocks, peers):
    slots = sens.shape[0]
    width = even.shape[2]
    piece = (blocks // peers, BLK, width)
    image = (RB_DEV, BLK, width)
    outs = pl.pallas_call(
        adjoint_body,
        out_shape=piece_shapes(piece, peers, jnp.bfloat16)
        + [jax.ShapeDtypeStruct(image, jnp.bfloat16)],
        in_specs=[SMEM_SPEC] * 4 + [ANY_SPEC] * 4,
        out_specs=[ANY_SPEC] * (peers // 2 + 2),
        scratch_shapes=[
            pltpu.VMEM(sens.shape, sens.dtype),
            pltpu.VMEM(image, jnp.bfloat16),
            pltpu.VMEM((blocks + 1, BLK, width), jnp.float32),
            pltpu.VMEM((peers, *piece), jnp.bfloat16),
            pltpu.SemaphoreType.DMA((slots // STEP,)),
            pltpu.SemaphoreType.DMA((peers,)),
            pltpu.SemaphoreType.DMA((peers,)),
            pltpu.SemaphoreType.DMA((4,)),
        ],
        compiler_params=pltpu.CompilerParams(vmem_limit_bytes=LARGE),
        cost_estimate=pl.CostEstimate(
            flops=2 * slots * BLK * BLK * width, bytes_accessed=2 * slots * BLK * BLK,
            transcendentals=0,
        ),
        name="adjoint",
    )(me, rows, cols, count, sens, even, odd, after)
    return outs[:-2], outs[-2], outs[-1]


def join_body(own_ref, other_ref, after_ref, out_ref, *, place):
    each = own_ref.shape[0]
    out_ref[:each] = own_ref[...]
    out_ref[each:] = other_ref[place * each : (place + 1) * each]


def join(own, other, place, after):
    each = own.shape[0]
    return pl.pallas_call(
        lambda *refs: join_body(*refs, place=place),
        out_shape=jax.ShapeDtypeStruct((2 * each, *own.shape[1:]), own.dtype),
        in_specs=[VMEM_SPEC, VMEM_SPEC, ANY_SPEC],
        out_specs=VMEM_SPEC,
        compiler_params=pltpu.CompilerParams(vmem_limit_bytes=SMALL),
        cost_estimate=pl.CostEstimate(
            flops=0, bytes_accessed=8 * own.size, transcendentals=0
        ),
        name="join",
    )(own, other, after)


def tile_value(near, face, window):
    span = lax.broadcasted_iota(jnp.int32, (2 * BLK, BLK), 0)
    center = lax.broadcasted_iota(jnp.int32, (2 * BLK, BLK), 1) + RIM
    mix = jnp.where(span == center, jnp.sum(face, axis=0, keepdims=True), 0.0)
    for k in range(4):
        mix = mix - jnp.where(span == near[k : k + 1], face[k : k + 1], 0.0)
    mix_high = mix.astype(jnp.bfloat16)
    mix_low = (mix - mix_high.astype(jnp.float32)).astype(jnp.bfloat16)
    near_high = window.astype(jnp.bfloat16)
    near_low = (window - near_high.astype(jnp.float32)).astype(jnp.bfloat16)
    return lax.dot_general(
        jnp.concatenate([mix_high, mix_high, mix_low], axis=0),
        jnp.concatenate([near_high, near_low, near_high], axis=0),
        (((0,), (0,)), ((), ())), preferred_element_type=jnp.float32,
    )


def smooth_body(offset_ref, model_ref, near_ref, weight_ref, after_ref,
                out_ref, ext_ref, value_ref, got, put):
    cells, width = model_ref.shape
    steps = put.shape[0]
    tiles = cells // BLK // steps
    each = cells // got.shape[0]
    loads = [
        pltpu.make_async_copy(
            model_ref.at[pl.ds(i * each, each)], ext_ref.at[pl.ds(RIM + i * each, each)], got.at[i]
        )
        for i in range(got.shape[0])
    ]
    start_all(loads)
    ext_ref[:RIM] = jnp.zeros((RIM, width), jnp.float32)
    ext_ref[RIM + cells :] = jnp.zeros((RIM, width), jnp.float32)
    wait_all(loads)

    def store(step):
        part = pl.ds(step * tiles * BLK, tiles * BLK)
        return pltpu.make_async_copy(value_ref.at[part], out_ref.at[part], put.at[step])

    @pl.loop(0, steps)
    def _(step):
        for t in range(tiles):
            start = pl.multiple_of((step * tiles + t) * BLK, BLK)
            near = near_ref[:, pl.ds(start, BLK)] - (offset_ref[0] + start)
            face = weight_ref[:, pl.ds(start, BLK)]
            window = ext_ref[pl.ds(start, 2 * BLK), :]
            value_ref[pl.ds(start, BLK), :] = tile_value(near, face, window)
        store(step).start()

    for step in range(steps):
        store(step).wait()


def smoothing(offset, model, neighbors, face_weight, after):
    cells, width = model.shape
    return pl.pallas_call(
        smooth_body,
        out_shape=jax.ShapeDtypeStruct((cells, width), jnp.float32),
        in_specs=[SMEM_SPEC, ANY_SPEC, VMEM_SPEC, VMEM_SPEC, ANY_SPEC],
        out_specs=ANY_SPEC,
        scratch_shapes=[
            pltpu.VMEM((cells + 2 * RIM, width), jnp.float32),
            pltpu.VMEM((cells, width), jnp.float32),
            pltpu.SemaphoreType.DMA((16,)),
            pltpu.SemaphoreType.DMA((8,)),
        ],
        compiler_params=pltpu.CompilerParams(vmem_limit_bytes=LARGE),
        cost_estimate=pl.CostEstimate(
            flops=24 * cells * BLK * width, bytes_accessed=16 * cells * width, transcendentals=0
        ),
        name="smoothing",
    )(offset, model, neighbors, face_weight, after)


def edges_body(offset_ref, low_ref, model_ref, high_ref, near_ref, weight_ref, base_ref, after_ref,
               out_ref, window_ref, value_ref, got, put):
    cells = model_ref.shape[0]
    inner = 2 * BLK - RIM
    starts = (0, cells - BLK)
    loads = [
        pltpu.make_async_copy(low_ref, window_ref.at[0, pl.ds(0, RIM)], got.at[0]),
        pltpu.make_async_copy(
            model_ref.at[pl.ds(0, inner)], window_ref.at[0, pl.ds(RIM, inner)], got.at[1]
        ),
        pltpu.make_async_copy(
            model_ref.at[pl.ds(cells - inner, inner)], window_ref.at[1, pl.ds(0, inner)], got.at[2]
        ),
        pltpu.make_async_copy(high_ref, window_ref.at[1, pl.ds(inner, RIM)], got.at[3]),
    ]
    start_all(loads)
    wait_all(loads)
    stores = []
    for i, start in enumerate(starts):
        near = near_ref[:, start : start + BLK] - (offset_ref[0] + start)
        value_ref[i] = tile_value(near, weight_ref[:, start : start + BLK], window_ref[i])
        stores.append(
            pltpu.make_async_copy(value_ref.at[i], out_ref.at[pl.ds(start, BLK)], put.at[i])
        )
    start_all(stores)
    wait_all(stores)


def edges(offset, low, model, high, neighbors, face_weight, base, after):
    width = model.shape[1]
    return pl.pallas_call(
        edges_body,
        out_shape=jax.ShapeDtypeStruct(base.shape, base.dtype),
        in_specs=[SMEM_SPEC, ANY_SPEC, ANY_SPEC, ANY_SPEC, VMEM_SPEC, VMEM_SPEC, ANY_SPEC, ANY_SPEC],
        out_specs=ANY_SPEC,
        input_output_aliases={6: 0},
        scratch_shapes=[
            pltpu.VMEM((2, 2 * BLK, width), jnp.float32),
            pltpu.VMEM((2, BLK, width), jnp.float32),
            pltpu.SemaphoreType.DMA((4,)),
            pltpu.SemaphoreType.DMA((2,)),
        ],
        compiler_params=pltpu.CompilerParams(vmem_limit_bytes=SMALL),
        cost_estimate=pl.CostEstimate(
            flops=24 * 2 * BLK * BLK * width, bytes_accessed=32 * BLK * width, transcendentals=0
        ),
        name="edges",
    )(offset, low, model, high, neighbors, face_weight, base, after)


def finish_body(me_ref, take_ref, order_ref, basis_ref, got_ref, mine_ref, base_ref, after_ref,
                out_ref, token_ref, block_ref, value_ref, got, put, *, offsets):
    cols = got_ref.shape[0]
    per_peer = cols // len(offsets)
    fetches, stores = [], []
    for i in range(cols):
        offset = offsets[i // per_peer]
        cell = order_ref[0, (me_ref[0] ^ offset) * per_peer + i % per_peer]
        fetches.append(pltpu.make_async_copy(base_ref.at[cell], block_ref.at[i], got.at[i]))
        stores.append(pltpu.make_async_copy(block_ref.at[i], out_ref.at[cell], put.at[i]))
    start_all(fetches)
    for i in range(cols):
        wave = jnp.where(take_ref[0] > 0, got_ref[i], mine_ref[i])
        both = jnp.concatenate([wave, wave], axis=0)
        value_ref[i] = jnp.dot(basis_ref[...], both, preferred_element_type=jnp.float32)
    wait_all(fetches)
    block_ref[...] += value_ref[...]
    start_all(stores)
    token_ref[...] = jnp.zeros_like(token_ref)
    wait_all(stores)


def finish(me, take, order, got, mine, base, after, offsets):
    cols, _, width = got.shape
    basis = haar_matrix(BLK).T.astype(np.float32)
    high = basis.astype(jnp.bfloat16)
    low = (basis - high.astype(np.float32)).astype(jnp.bfloat16)
    basis2 = jnp.asarray(np.concatenate([high, low], axis=1))
    return pl.pallas_call(
        lambda *refs: finish_body(*refs, offsets=offsets),
        out_shape=[
            jax.ShapeDtypeStruct(base.shape, base.dtype),
            jax.ShapeDtypeStruct((8, BLK), jnp.float32),
        ],
        in_specs=[SMEM_SPEC] * 3 + [VMEM_SPEC] * 3 + [ANY_SPEC] * 2,
        out_specs=[ANY_SPEC, VMEM_SPEC],
        input_output_aliases={6: 0},
        scratch_shapes=[
            pltpu.VMEM((cols, BLK, width), jnp.float32),
            pltpu.VMEM((cols, BLK, width), jnp.float32),
            pltpu.SemaphoreType.DMA((cols,)),
            pltpu.SemaphoreType.DMA((cols,)),
        ],
        compiler_params=pltpu.CompilerParams(vmem_limit_bytes=SMALL),
        cost_estimate=pl.CostEstimate(
            flops=4 * cols * BLK * BLK * width, bytes_accessed=10 * cols * BLK * width,
            transcendentals=0,
        ),
        name="finish",
    )(me, take, order, basis2, got, mine, base, after)


def merge_body(got_ref, mine_ref, after_ref, out_ref):
    total = got_ref[...].astype(jnp.float32) + mine_ref[...].astype(jnp.float32)
    out_ref[...] = total.astype(out_ref.dtype)


def merge(got, mine, after):
    return pl.pallas_call(
        merge_body,
        out_shape=jax.ShapeDtypeStruct(mine.shape, mine.dtype),
        in_specs=[VMEM_SPEC, VMEM_SPEC, ANY_SPEC],
        out_specs=VMEM_SPEC,
        compiler_params=pltpu.CompilerParams(vmem_limit_bytes=SMALL),
        cost_estimate=pl.CostEstimate(
            flops=mine.size, bytes_accessed=6 * mine.size, transcendentals=0
        ),
        name="merge",
    )(got, mine, after)


def line_sums(count_parts, make, axis, deliver):
    count = lax.axis_size(axis)
    half = count // 2
    me = lax.axis_index(axis)
    stages = []
    for hop in range(half - 1):
        stages.append(([(hop, hop + 1), (count - 1 - hop, count - 2 - hop)], False))
    stages.append(([(half - 1, half), (half, half - 1)], False))
    for hop in range(half - 1):
        left, right = half - 1 - hop, half + hop
        stages.append(([(left, left - 1), (right, right + 1)], True))
    state, got = [], []

    def add_part(after):
        if len(state) < count_parts:
            state.append(make(len(state), after))
            got.append(lax.ppermute(state[-1], axis, stages[0][0]))

    for _ in range(3):
        add_part(None)
    after = state[0]
    for time in range(count_parts + len(stages) - 1):
        for s, (pairs, outwards) in enumerate(stages):
            k = time - s
            if not 0 <= k < count_parts:
                continue
            last = s + 1 == len(stages)
            if outwards:
                take = (me == pairs[0][1]) | (me == pairs[1][1])
                take = take.astype(jnp.int32).reshape(1)
                if last:
                    after = deliver(k, take, got[k], state[k], after)
                else:
                    state[k] = jnp.where(take[0] > 0, got[k], state[k])
            else:
                state[k] = after = merge(got[k], state[k], after)
                if last:
                    after = deliver(k, jnp.zeros((1,), jnp.int32), state[k], state[k], after)
            if not last:
                got[k] = lax.ppermute(state[k], axis, stages[s + 1][0])
            if s == 0:
                add_part(after)


def halo(block, axis, width):
    count = lax.axis_size(axis)
    forward_pairs = [(i, i + 1) for i in range(count - 1)]
    backward_pairs = [(target, source) for source, target in forward_pairs]
    low = lax.ppermute(block[block.shape[0] - width :], axis, forward_pairs)
    high = lax.ppermute(block[:width], axis, backward_pairs)
    return low, high


def swap(piece, axis, offset):
    return lax.ppermute(piece, axis, [(c, c ^ offset) for c in range(lax.axis_size(axis))])


def local(model_dir, sens_blocks, blk_row, blk_col, blk_count, send_order, neighbors, face_weight):
    cell_count, width = model_dir.shape
    blocks = cell_count // BLK
    peers = lax.axis_size("cols")
    half = peers // 2
    per_peer = blocks // peers
    col = lax.axis_index("cols").astype(jnp.int32)
    me = col.reshape(1)
    offset = (col * cell_count - RIM).reshape(1)
    sens = sens_blocks[0]
    evens = range(1, half)

    *own, odd = analyze(me, send_order, model_dir.reshape(blocks, BLK, width), peers)
    partner = swap(odd, "cols", 1)
    direct = {j: swap(own[j], "cols", 2 * j) for j in reversed(evens)}
    passed = {
        j: swap(partner[j * per_peer : (j + 1) * per_peer], "cols", 2 * j)
        for j in reversed(evens)
    }
    waves = [own[0], partner]
    for j in evens:
        waves += [direct[j], passed[j]]
    smooth = smoothing(offset, model_dir, neighbors, face_weight, partner)

    even_rows, odd_rows = forward(
        me, blk_row, blk_col, blk_count, sens, waves, (smooth, blocks)
    )
    pair = (even_rows + swap(odd_rows, "cols", 1)).reshape(half, -1, BLK, width)
    to_send = pair.astype(jnp.bfloat16)
    shares = [swap(to_send[j], "cols", 2 * j) for j in evens]
    total = pair[0] + sum(share.astype(jnp.float32) for share in shares)
    image_share = total.astype(jnp.bfloat16)
    even_image = jnp.concatenate(
        [image_share] + [swap(image_share, "cols", 2 * j) for j in evens], axis=0
    )
    odd_image = swap(even_image, "cols", 1)

    own, odd, image = adjoint(
        me, blk_row, blk_col, blk_count, sens, even_image, odd_image, smooth, blocks, peers
    )
    data_image = image.reshape(RB_DEV * BLK, width).astype(jnp.float32)
    partner = swap(odd, "cols", 1)
    groups = [[0], [1]] + [[2 * j, 2 * j + 1] for j in evens]

    def make(chunk, after):
        if chunk == 0:
            return own[0]
        if chunk == 1:
            return partner[:per_peer]
        j = chunk - 1
        both = join(own[j], partner, j, own[0] if after is None else after)
        return swap(both, "cols", 2 * j)

    model_late, _ = lax.optimization_barrier((model_dir, own[0]))
    low, high = halo(model_late, "cols", RIM)
    smooth = edges(offset, low, model_dir, high, neighbors, face_weight, smooth, own[0])
    normal = smooth.reshape(blocks, BLK, width)

    def deliver(chunk, take, got, mine, after):
        nonlocal normal
        normal, token = finish(me, take, send_order, got, mine, normal, after, groups[chunk])
        return token

    line_sums(len(groups), make, "rows", deliver)
    return (data_image, normal.reshape(cell_count, width))


def solution(mesh):
    placed = (
        P("cols", None),
        P("rows", "cols", None, None),
        P("rows", "cols"),
        P("rows", "cols"),
        P("rows", "cols"),
        P("cols", None),
        P(None, "cols"),
        P(None, "cols"),
    )
    return jax.shard_map(
        local,
        mesh=mesh,
        in_specs=placed,
        out_specs=(P("rows", None), P("cols", None)),
        check_vma=False,
    )
```

profile of v0, /device:TPU:4, one launch (start us, length us, event | category | flops | bytes accessed | tf_op | source)
XLA Modules:
  0.0 198.4 jit_solution(7612930839092472021)
XLA Ops:
  0.6 5.0 %analyze.1 = (bf16[8,128,128]{2,1,0:T(8,128)(2,1)}, bf16[8,128,128]{2,1,0:T(8,128)(2,1)}, bf16[8,128,128]{2,1,0:T(8,128)(2,1)}, bf16[8,128,128]{2,1,0:T(8,128)(2,1)}, bf16[32,128,128]{2,1,0:T(8,128)(2,1)}) custom-call(s32[1]{0:T(128)} %bitcast.me_ref.refs_0_, s32[1,64]{1,0:T(1,128)} %refs_2_.9, f32[64,128,128]{2,1,0:T(8,128)} %bitcast.10), custom_call_target="tpu_custom_call" | custom-call | flops 536870912 | bytes 6291456 | tf_op jit(solution)/shard_map/analyze/pallas_call | solution.py:125
  5.7 1.6 collective-permute-start.1
  7.7 1.5 collective-permute-start.5
  10.0 1.6 collective-permute-start.2
  12.0 3.0 %collective-permute-done.1.refs_2_ = bf16[8,128,128]{2,1,0:T(8,128)(2,1)S(1)} collective-permute-done((bf16[8,128,128]{2,1,0:T(8,128)(2,1)}, bf16[8,128,128]{2,1,0:T(8,128)(2,1)S(1)}, u32[]{:S(2)}, u32[]{:S(2)}) %collective-permute-start.1) | collective-permute-done | bytes 262176 | tf_op jit(solution)/shard_map/ppermute | solution.py:559
  15.1 1.4 collective-permute-start.6
  16.5 13.3 %smoothing.1.refs_8_.after_ref.base_ref = f32[8192,128]{1,0:T(8,128)} custom-call(s32[1]{0:T(128)} %bitcast.3.offset_ref, f32[8192,128]{1,0:T(8,128)} %model_ref.3, s32[4,8192]{1,0:T(4,128)} %near_ref.3, f32[4,8192]{1,0:T(4,128)} %weight_ref.3, bf16[32,128,128]{2,1,0:T(8,128)(2,1)} %copy-done.14), custom_call_target="tpu_custom_call" | custom-call | flops 3221225472 | bytes 16777216 | tf_op jit(solution)/shard_map/smoothing/pallas_call | solution.py:365
  29.9 2.8 %collective-permute-done.4.refs_5_ = bf16[8,128,128]{2,1,0:T(8,128)(2,1)S(1)} collective-permute-done((bf16[8,128,128]{2,1,0:T(8,128)(2,1)S(1)}, bf16[8,128,128]{2,1,0:T(8,128)(2,1)S(1)}, u32[]{:S(2)}, u32[]{:S(2)}) %collective-permute-start.4) | collective-permute-done | bytes 262176 | tf_op jit(solution)/shard_map/ppermute | solution.py:559
  33.5 5.4 %forward.1 = (f32[16,128,128]{2,1,0:T(8,128)}, f32[16,128,128]{2,1,0:T(8,128)}) custom-call(s32[1]{0:T(128)} %bitcast.me_ref.refs_0_, s32[1,384]{1,0:T(1,128)} %rows_ref.3, s32[1,384]{1,0:T(1,128)} %cols_ref.3, s32[1,1]{1,0:T(1,128)S(6)} %copy.27.count_ref, bf16[384,128,128]{2,1,0:T(8,128)(2,1)} %bitcast.13, bf16[8,128,128]{2,1,0:T(8,128)(2,1)} %get-tuple-element.25.refs_0_, ...), custom_call_target="tpu_custom_call" | custom-call | flops 1610612736 | bytes 12582912 | tf_op jit(solution)/shard_map/forward/pallas_call | solution.py:206
  38.9 2.9 %collective-permute-done.7 = f32[16,128,128]{2,1,0:T(8,128)S(1)} collective-permute-done((f32[16,128,128]{2,1,0:T(8,128)}, f32[16,128,128]{2,1,0:T(8,128)S(1)}, u32[]{:S(2)}, u32[]{:S(2)}) %collective-permute-start.7) | collective-permute-done | bytes 1048608 | tf_op jit(solution)/shard_map/ppermute | solution.py:559
  41.8 1.4 fusion.1
  43.2 7.1 %collective-permute-start.10 = (bf16[4,128,128]{2,1,0:T(8,128)(2,1)S(1)}, bf16[4,128,128]{2,1,0:T(8,128)(2,1)S(1)}, u32[]{:S(2)}, u32[]{:S(2)}) collective-permute-start(bf16[4,128,128]{2,1,0:T(8,128)(2,1)S(1)} %get-tuple-element.56), channel_id=1, source_target_pairs={{0,6},{1,7},{2,4},{3,5},{4,2},{5,3},{6,0},{7,1},{8,14},{9,15},{10,... | collective-permute-start | bytes 393224 | tf_op jit(solution)/shard_map/ppermute | solution.py:559
  51.0 3.6 %collective-permute-done.10 = bf16[4,128,128]{2,1,0:T(8,128)(2,1)S(1)} collective-permute-done((bf16[4,128,128]{2,1,0:T(8,128)(2,1)S(1)}, bf16[4,128,128]{2,1,0:T(8,128)(2,1)S(1)}, u32[]{:S(2)}, u32[]{:S(2)}) %collective-permute-start.10) | collective-permute-done | bytes 131104 | tf_op jit(solution)/shard_map/ppermute | solution.py:559
  54.7 1.6 collective-permute-done.8
  56.3 0.7 collective-permute-done.9
  57.1 1.8 collective-permute-start.11
  58.9 1.4 collective-permute-start.12
  60.6 2.3 %collective-permute-done.11 = bf16[4,128,128]{2,1,0:T(8,128)(2,1)S(1)} collective-permute-done((bf16[4,128,128]{2,1,0:T(8,128)(2,1)S(1)}, bf16[4,128,128]{2,1,0:T(8,128)(2,1)S(1)}, u32[]{:S(2)}, u32[]{:S(2)}) %collective-permute-start.11) | collective-permute-done | bytes 131104 | tf_op jit(solution)/shard_map/ppermute | solution.py:559
  62.9 3.8 %collective-permute-done.12 = bf16[4,128,128]{2,1,0:T(8,128)(2,1)S(1)} collective-permute-done((bf16[4,128,128]{2,1,0:T(8,128)(2,1)S(1)}, bf16[4,128,128]{2,1,0:T(8,128)(2,1)S(1)}, u32[]{:S(2)}, u32[]{:S(2)}) %collective-permute-start.12) | collective-permute-done | bytes 131104 | tf_op jit(solution)/shard_map/ppermute | solution.py:559
  66.8 1.9 collective-permute-done.14.odd_in_ref
  68.7 0.8 copy-done.17
  69.5 5.7 %adjoint.1 = (bf16[8,128,128]{2,1,0:T(8,128)(2,1)}, bf16[8,128,128]{2,1,0:T(8,128)(2,1)}, bf16[8,128,128]{2,1,0:T(8,128)(2,1)}, bf16[8,128,128]{2,1,0:T(8,128)(2...) custom-call(s32[1]{0:T(128)} %bitcast.me_ref.refs_0_, s32[1,384]{1,0:T(1,128)} %rows_ref.3, ...), custom_call_target="tpu_custom_call" | custom-call | flops 1610612736 | bytes 12582912 | tf_op jit(solution)/shard_map/adjoint/pallas_call | solution.py:264
  75.8 2.5 %collective-permute-done.15.refs_1_ = bf16[32,128,128]{2,1,0:T(8,128)(2,1)S(1)} collective-permute-done((bf16[32,128,128]{2,1,0:T(8,128)(2,1)}, bf16[32,128,128]{2,1,0:T(8,128)(2,1)S(1)}, u32[]{:S(2)}, u32[]{:S(2)}) %collective-permute-start.15) | collective-permute-done | bytes 1048608 | tf_op jit(solution)/shard_map/ppermute | solution.py:559
  78.3 0.9 copy-done.1
  79.2 0.9 copy-done.6
  80.2 3.3 %collective-permute-start.21 = (bf16[16,128,128]{2,1,0:T(8,128)(2,1)S(1)}, bf16[16,128,128]{2,1,0:T(8,128)(2,1)S(1)}, u32[]{:S(2)}, u32[]{:S(2)}) collective-permute-start(bf16[16,128,128]{2,1,0:T(8,128)(2,1)S(1)} %join.4), channel_id=1, source_target_pairs={{0,2},{1,3},{2,0},{3,1},{4,6},{5,7},{6,4},{7,5},{8,10},{9,11},{10,... | collective-permute-start | bytes 1572872 | tf_op jit(solution)/shard_map/ppermute | solution.py:559
  83.6 3.4 %collective-permute-start.17 = (bf16[8,128,128]{2,1,0:T(8,128)(2,1)S(1)}, bf16[8,128,128]{2,1,0:T(8,128)(2,1)S(1)}, u32[]{:S(2)}, u32[]{:S(2)}) collective-permute-start(bf16[8,128,128]{2,1,0:T(8,128)(2,1)S(1)} %copy-done.1), channel_id=1, source_target_pairs={{0,8},{24,16},{1,9},{25,17},{2,10},{26,18},{3,11},{27,19},{4,12},{... | collective-permute-start | bytes 786440 | tf_op jit(solution)/shard_map/ppermute | solution.py:521
  87.0 1.3 collective-permute-start.16
  88.3 5.3 %collective-permute-done.17.got_ref = bf16[8,128,128]{2,1,0:T(8,128)(2,1)S(1)} collective-permute-done((bf16[8,128,128]{2,1,0:T(8,128)(2,1)S(1)}, bf16[8,128,128]{2,1,0:T(8,128)(2,1)S(1)}, u32[]{:S(2)}, u32[]{:S(2)}) %collective-permute-start.17) | collective-permute-done | bytes 262176 | tf_op jit(solution)/shard_map/ppermute | solution.py:521
  93.7 0.9 copy-done.5
  94.7 3.8 %collective-permute-start.29 = (bf16[16,128,128]{2,1,0:T(8,128)(2,1)S(1)}, bf16[16,128,128]{2,1,0:T(8,128)(2,1)S(1)}, u32[]{:S(2)}, u32[]{:S(2)}) collective-permute-start(bf16[16,128,128]{2,1,0:T(8,128)(2,1)S(1)} %join.5), channel_id=1, source_target_pairs={{0,4},{1,5},{2,6},{3,7},{4,0},{5,1},{6,2},{7,3},{8,12},{9,13},{10,... | collective-permute-start | bytes 1572872 | tf_op jit(solution)/shard_map/ppermute | solution.py:559
  98.6 5.1 %collective-permute-start.18 = (bf16[16,128,128]{2,1,0:T(8,128)(2,1)S(1)}, bf16[16,128,128]{2,1,0:T(8,128)(2,1)S(1)}, u32[]{:S(2)}, u32[]{:S(2)}) collective-permute-start(bf16[16,128,128]{2,1,0:T(8,128)(2,1)S(1)} %join.3), channel_id=1, source_target_pairs={{0,6},{1,7},{2,4},{3,5},{4,2},{5,3},{6,0},{7,1},{8,14},{9,15},{10,... | collective-permute-start | bytes 1572872 | tf_op jit(solution)/shard_map/ppermute | solution.py:559
  103.7 4.4 %collective-permute-start.22 = (bf16[16,128,128]{2,1,0:T(8,128)(2,1)S(1)}, bf16[16,128,128]{2,1,0:T(8,128)(2,1)S(1)}, u32[]{:S(2)}, u32[]{:S(2)}) collective-permute-start(bf16[16,128,128]{2,1,0:T(8,128)(2,1)S(1)} %collective-permute-done.21.mine_ref), channel_id=1, source_target_pairs={{0,8},{24,16},{1,9},{25,17},{2,10},{26,18},{3,11},{27,19},{4,12},{... | collective-permute-start | bytes 1572872 | tf_op jit(solution)/shard_map/ppermute | solution.py:521
  109.6 11.2 %collective-permute-done.29.mine_ref = bf16[16,128,128]{2,1,0:T(8,128)(2,1)S(1)} collective-permute-done((bf16[16,128,128]{2,1,0:T(8,128)(2,1)S(1)}, bf16[16,128,128]{2,1,0:T(8,128)(2,1)S(1)}, u32[]{:S(2)}, u32[]{:S(2)}) %collective-permute-start.29) | collective-permute-done | bytes 524320 | tf_op jit(solution)/shard_map/ppermute | solution.py:559
  120.8 4.4 %collective-permute-start.30 = (bf16[16,128,128]{2,1,0:T(8,128)(2,1)S(1)}, bf16[16,128,128]{2,1,0:T(8,128)(2,1)S(1)}, u32[]{:S(2)}, u32[]{:S(2)}) collective-permute-start(bf16[16,128,128]{2,1,0:T(8,128)(2,1)S(1)} %collective-permute-done.29.mine_ref), channel_id=1, source_target_pairs={{0,8},{24,16},{1,9},{25,17},{2,10},{26,18},{3,11},{27,19},{4,12},{... | collective-permute-start | bytes 1572872 | tf_op jit(solution)/shard_map/ppermute | solution.py:521
  125.2 1.3 collective-permute-start.19
  126.7 1.5 collective-permute-start.28
  128.1 0.8 fusion.2
  128.9 1.9 collective-permute-start.26
  130.8 4.2 %collective-permute-done.26.low_ref = f32[64,128]{1,0:T(8,128)S(1)} collective-permute-done((f32[64,128]{1,0:T(8,128)S(1)}, f32[64,128]{1,0:T(8,128)S(1)}, u32[]{:S(2)}, u32[]{:S(2)}) %collective-permute-start.26) | collective-permute-done | bytes 32800 | tf_op jit(solution)/shard_map/ppermute | solution.py:553
  135.7 1.9 collective-permute-start.27
  137.6 1.3 collective-permute-start.25
  139.8 1.3 collective-permute-start.24
  141.1 2.2 %copy-done = f32[8192,128]{1,0:T(8,128)S(1)} copy-done((f32[8192,128]{1,0:T(8,128)S(1)}, f32[8192,128]{1,0:T(8,128)}, u32[]{:S(2)}) %copy-start) | copy-done | bytes 4194328
  143.3 0.9 copy-done.8
  144.2 0.8 copy-done.10
  144.9 0.8 copy-done.12
  145.7 1.4 edges.1
  147.1 1.6 collective-permute-done.25.refs_4_
  148.7 3.1 %finish.5 = (f32[64,128,128]{2,1,0:T(8,128)}, f32[8,128]{1,0:T(8,128)S(1)}) custom-call(s32[1]{0:T(128)} %bitcast.me_ref.refs_0_, s32[1]{0:T(128)} %bitcast.5.refs_1_, s32[1,64]{1,0:T(1,128)S(1)} %copy-done.13, bf16[128,256]{1,0:T(8,128)(2,1)S(1)} %copy-done.3, ...), custom_call_target="tpu_custom_call", output_to_operand_aliasing={{0}: (6, {})} | custom-call | flops 67108864 | bytes 1310720 | tf_op jit(solution)/shard_map/finish/pallas_call | solution.py:462
  151.9 0.7 collective-permute-start.33
  152.6 1.2 merge.16.refs_7_.refs_5_
  153.8 1.3 collective-permute-start.32
  155.1 3.1 %finish.6 = (f32[64,128,128]{2,1,0:T(8,128)}, f32[8,128]{1,0:T(8,128)S(1)}) custom-call(s32[1]{0:T(128)} %bitcast.me_ref.refs_0_, s32[1]{0:T(128)} %bitcast.5.refs_1_, s32[1,64]{1,0:T(1,128)S(1)} %copy-done.13, bf16[128,256]{1,0:T(8,128)(2,1)S(1)} %copy-done.3, ...), custom_call_target="tpu_custom_call", output_to_operand_aliasing={{0}: (6, {})} | custom-call | flops 67108864 | bytes 1310720 | tf_op jit(solution)/shard_map/finish/pallas_call | solution.py:462
  158.3 0.7 collective-permute-start.31
  159.2 1.4 collective-permute-start.35
  160.6 10.3 %collective-permute-done.32.refs_4_ = bf16[16,128,128]{2,1,0:T(8,128)(2,1)S(1)} collective-permute-done((bf16[16,128,128]{2,1,0:T(8,128)(2,1)S(1)}, bf16[16,128,128]{2,1,0:T(8,128)(2,1)S(1)}, u32[]{:S(2)}, u32[]{:S(2)}) %collective-permute-start.32) | collective-permute-done | bytes 524320 | tf_op jit(solution)/shard_map/ppermute | solution.py:544
  170.9 3.4 %finish.7 = (f32[64,128,128]{2,1,0:T(8,128)}, f32[8,128]{1,0:T(8,128)S(1)}) custom-call(s32[1]{0:T(128)} %bitcast.me_ref.refs_0_, s32[1]{0:T(128)} %bitcast.5.refs_1_, s32[1,64]{1,0:T(1,128)S(1)} %copy-done.13, bf16[128,256]{1,0:T(8,128)(2,1)S(1)} %copy-done.3, ...), custom_call_target="tpu_custom_call", output_to_operand_aliasing={{0}: (6, {})} | custom-call | flops 134217728 | bytes 2621440 | tf_op jit(solution)/shard_map/finish/pallas_call | solution.py:462
  174.4 1.3 collective-permute-start.34
  175.7 1.5 bitcast_convert_fusion
  177.2 6.1 %collective-permute-done.35.refs_4_ = bf16[16,128,128]{2,1,0:T(8,128)(2,1)S(1)} collective-permute-done((bf16[16,128,128]{2,1,0:T(8,128)(2,1)S(1)}, bf16[16,128,128]{2,1,0:T(8,128)(2,1)S(1)}, u32[]{:S(2)}, u32[]{:S(2)}) %collective-permute-start.35) | collective-permute-done | bytes 524320 | tf_op jit(solution)/shard_map/ppermute | solution.py:544
  183.3 3.4 %finish.8 = (f32[64,128,128]{2,1,0:T(8,128)}, f32[8,128]{1,0:T(8,128)S(1)}) custom-call(s32[1]{0:T(128)} %bitcast.me_ref.refs_0_, s32[1]{0:T(128)} %bitcast.5.refs_1_, s32[1,64]{1,0:T(1,128)S(1)} %copy-done.13, bf16[128,256]{1,0:T(8,128)(2,1)S(1)} %copy-done.3, ...), custom_call_target="tpu_custom_call", output_to_operand_aliasing={{0}: (6, {})} | custom-call | flops 134217728 | bytes 2621440 | tf_op jit(solution)/shard_map/finish/pallas_call | solution.py:462
  186.7 7.8 %collective-permute-done.34.refs_4_ = bf16[16,128,128]{2,1,0:T(8,128)(2,1)S(1)} collective-permute-done((bf16[16,128,128]{2,1,0:T(8,128)(2,1)S(1)}, bf16[16,128,128]{2,1,0:T(8,128)(2,1)S(1)}, u32[]{:S(2)}, u32[]{:S(2)}) %collective-permute-start.34) | collective-permute-done | bytes 524320 | tf_op jit(solution)/shard_map/ppermute | solution.py:544
  194.4 3.9 %finish.9 = (f32[64,128,128]{2,1,0:T(8,128)}, f32[8,128]{1,0:T(8,128)}) custom-call(s32[1]{0:T(128)} %bitcast.me_ref.refs_0_, s32[1]{0:T(128)} %bitcast.5.refs_1_, s32[1,64]{1,0:T(1,128)S(1)} %copy-done.13, bf16[128,256]{1,0:T(8,128)(2,1)S(1)} %copy-done.3, ...), custom_call_target="tpu_custom_call", output_to_operand_aliasing={{0}: (6, {})} | custom-call | flops 134217728 | bytes 2621440 | tf_op jit(solution)/shard_map/finish/pallas_call | solution.py:462
  (87 shorter events, 7.6 us)
Async XLA Ops:
  5.6 4.3 %collective-permute-start = (bf16[32,128,128]{2,1,0:T(8,128)(2,1)}, bf16[32,128,128]{2,1,0:T(8,128)(2,1)S(1)}, u32[]{:S(2)}, u32[]{:S(2)}) collective-permute-start(bf16[32,128,128]{2,1,0:T(8,128)(2,1)} %get-tuple-element.26), channel_id=1, source_target_pairs={{0,1},{1,0},{2,3},{3,2},{4,5},{5,4},{6,7},{7,6},{8,9},{9,8},{10,11... | collective-permute-start | bytes 3145736 | tf_op jit(solution)/shard_map/ppermute | solution.py:559
  5.7 9.4 %collective-permute-start.1 = (bf16[8,128,128]{2,1,0:T(8,128)(2,1)}, bf16[8,128,128]{2,1,0:T(8,128)(2,1)S(1)}, u32[]{:S(2)}, u32[]{:S(2)}) collective-permute-start(bf16[8,128,128]{2,1,0:T(8,128)(2,1)} %get-tuple-element.27), channel_id=1, source_target_pairs={{0,2},{1,3},{2,0},{3,1},{4,6},{5,7},{6,4},{7,5},{8,10},{9,11},{10,... | collective-permute-start | bytes 786440 | tf_op jit(solution)/shard_map/ppermute | solution.py:559
  7.2 22.6 %collective-permute-start.3 = (bf16[8,128,128]{2,1,0:T(8,128)(2,1)}, bf16[8,128,128]{2,1,0:T(8,128)(2,1)S(1)}, u32[]{:S(2)}, u32[]{:S(2)}) collective-permute-start(bf16[8,128,128]{2,1,0:T(8,128)(2,1)} %get-tuple-element.28), channel_id=1, source_target_pairs={{0,4},{1,5},{2,6},{3,7},{4,0},{5,1},{6,2},{7,3},{8,12},{9,13},{10,... | collective-permute-start | bytes 786440 | tf_op jit(solution)/shard_map/ppermute | solution.py:559
  7.7 22.1 %collective-permute-start.5 = (bf16[8,128,128]{2,1,0:T(8,128)(2,1)}, bf16[8,128,128]{2,1,0:T(8,128)(2,1)S(1)}, u32[]{:S(2)}, u32[]{:S(2)}) collective-permute-start(bf16[8,128,128]{2,1,0:T(8,128)(2,1)} %get-tuple-element.29), channel_id=1, source_target_pairs={{0,6},{1,7},{2,4},{3,5},{4,2},{5,3},{6,0},{7,1},{8,14},{9,15},{10,... | collective-permute-start | bytes 786440 | tf_op jit(solution)/shard_map/ppermute | solution.py:559
  9.9 6.6 %copy-start.14 = (bf16[32,128,128]{2,1,0:T(8,128)(2,1)}, bf16[32,128,128]{2,1,0:T(8,128)(2,1)S(1)}, u32[]{:S(2)}) copy-start(bf16[32,128,128]{2,1,0:T(8,128)(2,1)S(1)} %collective-permute-done.after_ref.refs_1_) | copy-start | bytes 3145732
  10.0 19.9 %collective-permute-start.2 = (bf16[8,128,128]{2,1,0:T(8,128)(2,1)S(1)}, bf16[8,128,128]{2,1,0:T(8,128)(2,1)S(1)}, u32[]{:S(2)}, u32[]{:S(2)}) collective-permute-start(bf16[8,128,128]{2,1,0:T(8,128)(2,1)S(1)} %get-tuple-element.54), channel_id=1, source_target_pairs={{0,2},{1,3},{2,0},{3,1},{4,6},{5,7},{6,4},{7,5},{8,10},{9,11},{10,... | collective-permute-start | bytes 786440 | tf_op jit(solution)/shard_map/ppermute | solution.py:559
  11.5 21.1 %collective-permute-start.4 = (bf16[8,128,128]{2,1,0:T(8,128)(2,1)S(1)}, bf16[8,128,128]{2,1,0:T(8,128)(2,1)S(1)}, u32[]{:S(2)}, u32[]{:S(2)}) collective-permute-start(bf16[8,128,128]{2,1,0:T(8,128)(2,1)S(1)} %get-tuple-element.53), channel_id=1, source_target_pairs={{0,4},{1,5},{2,6},{3,7},{4,0},{5,1},{6,2},{7,3},{8,12},{9,13},{10,... | collective-permute-start | bytes 786440 | tf_op jit(solution)/shard_map/ppermute | solution.py:559
  15.1 14.8 %copy-start.18 = (bf16[8,128,128]{2,1,0:T(8,128)(2,1)}, bf16[8,128,128]{2,1,0:T(8,128)(2,1)S(1)}, u32[]{:S(2)}) copy-start(bf16[8,128,128]{2,1,0:T(8,128)(2,1)S(1)} %collective-permute-done.1.refs_2_) | copy-start | bytes 786436
  15.1 17.6 %collective-permute-start.6 = (bf16[8,128,128]{2,1,0:T(8,128)(2,1)S(1)}, bf16[8,128,128]{2,1,0:T(8,128)(2,1)S(1)}, u32[]{:S(2)}, u32[]{:S(2)}) collective-permute-start(bf16[8,128,128]{2,1,0:T(8,128)(2,1)S(1)} %get-tuple-element.52), channel_id=1, source_target_pairs={{0,6},{1,7},{2,4},{3,5},{4,2},{5,3},{6,0},{7,1},{8,14},{9,15},{10,... | collective-permute-start | bytes 786440 | tf_op jit(solution)/shard_map/ppermute | solution.py:559
  29.8 2.9 %copy-start.19 = (bf16[8,128,128]{2,1,0:T(8,128)(2,1)}, bf16[8,128,128]{2,1,0:T(8,128)(2,1)S(1)}, u32[]{:S(2)}) copy-start(bf16[8,128,128]{2,1,0:T(8,128)(2,1)S(1)} %collective-permute-done.3.refs_4_) | copy-start | bytes 786436
  29.9 2.8 %copy-start.20 = (bf16[8,128,128]{2,1,0:T(8,128)(2,1)}, bf16[8,128,128]{2,1,0:T(8,128)(2,1)S(1)}, u32[]{:S(2)}) copy-start(bf16[8,128,128]{2,1,0:T(8,128)(2,1)S(1)} %collective-permute-done.5.refs_6_) | copy-start | bytes 786436
  29.9 2.8 %copy-start.21 = (bf16[8,128,128]{2,1,0:T(8,128)(2,1)}, bf16[8,128,128]{2,1,0:T(8,128)(2,1)S(1)}, u32[]{:S(2)}) copy-start(bf16[8,128,128]{2,1,0:T(8,128)(2,1)S(1)} %collective-permute-done.2.refs_3_) | copy-start | bytes 786436
  32.7 0.7 copy-start.22
  32.7 0.8 copy-start.23
  38.9 2.9 %collective-permute-start.7 = (f32[16,128,128]{2,1,0:T(8,128)}, f32[16,128,128]{2,1,0:T(8,128)S(1)}, u32[]{:S(2)}, u32[]{:S(2)}) collective-permute-start(f32[16,128,128]{2,1,0:T(8,128)} %get-tuple-element.31), channel_id=1, source_target_pairs={{0,1},{1,0},{2,3},{3,2},{4,5},{5,4},{6,7},{7,6},{8,9},{9,8},{10,11... | collective-permute-start | bytes 3145736 | tf_op jit(solution)/shard_map/ppermute | solution.py:559
  43.2 11.4 %collective-permute-start.10 = (bf16[4,128,128]{2,1,0:T(8,128)(2,1)S(1)}, bf16[4,128,128]{2,1,0:T(8,128)(2,1)S(1)}, u32[]{:S(2)}, u32[]{:S(2)}) collective-permute-start(bf16[4,128,128]{2,1,0:T(8,128)(2,1)S(1)} %get-tuple-element.56), channel_id=1, source_target_pairs={{0,6},{1,7},{2,4},{3,5},{4,2},{5,3},{6,0},{7,1},{8,14},{9,15},{10,... | collective-permute-start | bytes 393224 | tf_op jit(solution)/shard_map/ppermute | solution.py:559
  50.4 5.9 %collective-permute-start.8 = (bf16[4,128,128]{2,1,0:T(8,128)(2,1)S(1)}, bf16[4,128,128]{2,1,0:T(8,128)(2,1)S(1)}, u32[]{:S(2)}, u32[]{:S(2)}) collective-permute-start(bf16[4,128,128]{2,1,0:T(8,128)(2,1)S(1)} %get-tuple-element.55), channel_id=1, source_target_pairs={{0,2},{1,3},{2,0},{3,1},{4,6},{5,7},{6,4},{7,5},{8,10},{9,11},{10,... | collective-permute-start | bytes 393224 | tf_op jit(solution)/shard_map/ppermute | solution.py:559
  50.4 6.6 %collective-permute-start.9 = (bf16[4,128,128]{2,1,0:T(8,128)(2,1)S(1)}, bf16[4,128,128]{2,1,0:T(8,128)(2,1)S(1)}, u32[]{:S(2)}, u32[]{:S(2)}) collective-permute-start(bf16[4,128,128]{2,1,0:T(8,128)(2,1)S(1)} %get-tuple-element.57), channel_id=1, source_target_pairs={{0,4},{1,5},{2,6},{3,7},{4,0},{5,1},{6,2},{7,3},{8,12},{9,13},{10,... | collective-permute-start | bytes 393224 | tf_op jit(solution)/shard_map/ppermute | solution.py:559
  57.1 5.8 %collective-permute-start.11 = (bf16[4,128,128]{2,1,0:T(8,128)(2,1)S(1)}, bf16[4,128,128]{2,1,0:T(8,128)(2,1)S(1)}, u32[]{:S(2)}, u32[]{:S(2)}) collective-permute-start(bf16[4,128,128]{2,1,0:T(8,128)(2,1)S(1)} %fusion), channel_id=1, source_target_pairs={{0,2},{1,3},{2,0},{3,1},{4,6},{5,7},{6,4},{7,5},{8,10},{9,11},{10,... | collective-permute-start | bytes 393224 | tf_op jit(solution)/shard_map/ppermute | solution.py:559
  58.9 7.8 %collective-permute-start.12 = (bf16[4,128,128]{2,1,0:T(8,128)(2,1)S(1)}, bf16[4,128,128]{2,1,0:T(8,128)(2,1)S(1)}, u32[]{:S(2)}, u32[]{:S(2)}) collective-permute-start(bf16[4,128,128]{2,1,0:T(8,128)(2,1)S(1)} %fusion), channel_id=1, source_target_pairs={{0,4},{1,5},{2,6},{3,7},{4,0},{5,1},{6,2},{7,3},{8,12},{9,13},{10,... | collective-permute-start | bytes 393224 | tf_op jit(solution)/shard_map/ppermute | solution.py:559
  60.3 6.3 %collective-permute-start.13 = (bf16[4,128,128]{2,1,0:T(8,128)(2,1)S(1)}, bf16[4,128,128]{2,1,0:T(8,128)(2,1)S(1)}, u32[]{:S(2)}, u32[]{:S(2)}) collective-permute-start(bf16[4,128,128]{2,1,0:T(8,128)(2,1)S(1)} %fusion), channel_id=1, source_target_pairs={{0,6},{1,7},{2,4},{3,5},{4,2},{5,3},{6,0},{7,1},{8,14},{9,15},{10,... | collective-permute-start | bytes 393224 | tf_op jit(solution)/shard_map/ppermute | solution.py:559
  66.8 2.0 %copy-start.15 = (bf16[16,128,128]{2,1,0:T(8,128)(2,1)}, bf16[16,128,128]{2,1,0:T(8,128)(2,1)S(1)}, u32[]{:S(2)}) copy-start(bf16[16,128,128]{2,1,0:T(8,128)(2,1)S(1)} %pad_maximum_fusion.even_in_ref) | copy-start | bytes 1572868
  66.8 2.0 collective-permute-start.14
  68.7 0.8 copy-start.17
  75.2 3.0 %collective-permute-start.15 = (bf16[32,128,128]{2,1,0:T(8,128)(2,1)}, bf16[32,128,128]{2,1,0:T(8,128)(2,1)S(1)}, u32[]{:S(2)}, u32[]{:S(2)}) collective-permute-start(bf16[32,128,128]{2,1,0:T(8,128)(2,1)} %get-tuple-element.34), channel_id=1, source_target_pairs={{0,1},{1,0},{2,3},{3,2},{4,5},{5,4},{6,7},{7,6},{8,9},{9,8},{10,11... | collective-permute-start | bytes 3145736 | tf_op jit(solution)/shard_map/ppermute | solution.py:559
  78.3 0.9 copy-start.1
  79.2 0.9 copy-start.6
  80.2 18.4 %copy-start.4 = (bf16[8,128,128]{2,1,0:T(8,128)(2,1)S(1)}, bf16[8,128,128]{2,1,0:T(8,128)(2,1)}, u32[]{:S(2)}) copy-start(bf16[8,128,128]{2,1,0:T(8,128)(2,1)} %get-tuple-element.33.refs_0_) | copy-start | bytes 786436
  80.2 23.5 %collective-permute-start.21 = (bf16[16,128,128]{2,1,0:T(8,128)(2,1)S(1)}, bf16[16,128,128]{2,1,0:T(8,128)(2,1)S(1)}, u32[]{:S(2)}, u32[]{:S(2)}) collective-permute-start(bf16[16,128,128]{2,1,0:T(8,128)(2,1)S(1)} %join.4), channel_id=1, source_target_pairs={{0,2},{1,3},{2,0},{3,1},{4,6},{5,7},{6,4},{7,5},{8,10},{9,11},{10,... | collective-permute-start | bytes 1572872 | tf_op jit(solution)/shard_map/ppermute | solution.py:559
  83.6 10.1 %collective-permute-start.17 = (bf16[8,128,128]{2,1,0:T(8,128)(2,1)S(1)}, bf16[8,128,128]{2,1,0:T(8,128)(2,1)S(1)}, u32[]{:S(2)}, u32[]{:S(2)}) collective-permute-start(bf16[8,128,128]{2,1,0:T(8,128)(2,1)S(1)} %copy-done.1), channel_id=1, source_target_pairs={{0,8},{24,16},{1,9},{25,17},{2,10},{26,18},{3,11},{27,19},{4,12},{... | collective-permute-start | bytes 786440 | tf_op jit(solution)/shard_map/ppermute | solution.py:521
  87.0 11.5 %collective-permute-start.16 = (bf16[8,128,128]{2,1,0:T(8,128)(2,1)S(1)}, bf16[8,128,128]{2,1,0:T(8,128)(2,1)S(1)}, u32[]{:S(2)}, u32[]{:S(2)}) collective-permute-start(bf16[8,128,128]{2,1,0:T(8,128)(2,1)S(1)} %slice.51.mine_ref), channel_id=1, source_target_pairs={{0,8},{24,16},{1,9},{25,17},{2,10},{26,18},{3,11},{27,19},{4,12},{... | collective-permute-start | bytes 786440 | tf_op jit(solution)/shard_map/ppermute | solution.py:521
  93.7 1.0 copy-start.5
  94.7 46.4 %copy-start.2 = (bf16[8,128,128]{2,1,0:T(8,128)(2,1)S(1)}, bf16[8,128,128]{2,1,0:T(8,128)(2,1)}, u32[]{:S(2)}) copy-start(bf16[8,128,128]{2,1,0:T(8,128)(2,1)} %get-tuple-element.35.mine_ref.after_ref.refs_2_) | copy-start | bytes 786436
  94.7 46.4 %copy-start.7 = (s32[4,8192]{1,0:T(4,128)S(1)}, s32[4,8192]{1,0:T(4,128)}, u32[]{:S(2)}) copy-start(s32[4,8192]{1,0:T(4,128)} %near_ref.3) | copy-start | bytes 393220
  94.7 26.1 %collective-permute-start.29 = (bf16[16,128,128]{2,1,0:T(8,128)(2,1)S(1)}, bf16[16,128,128]{2,1,0:T(8,128)(2,1)S(1)}, u32[]{:S(2)}, u32[]{:S(2)}) collective-permute-start(bf16[16,128,128]{2,1,0:T(8,128)(2,1)S(1)} %join.5), channel_id=1, source_target_pairs={{0,4},{1,5},{2,6},{3,7},{4,0},{5,1},{6,2},{7,3},{8,12},{9,13},{10,... | collective-permute-start | bytes 1572872 | tf_op jit(solution)/shard_map/ppermute | solution.py:559
  98.6 26.6 %collective-permute-start.18 = (bf16[16,128,128]{2,1,0:T(8,128)(2,1)S(1)}, bf16[16,128,128]{2,1,0:T(8,128)(2,1)S(1)}, u32[]{:S(2)}, u32[]{:S(2)}) collective-permute-start(bf16[16,128,128]{2,1,0:T(8,128)(2,1)S(1)} %join.3), channel_id=1, source_target_pairs={{0,6},{1,7},{2,4},{3,5},{4,2},{5,3},{6,0},{7,1},{8,14},{9,15},{10,... | collective-permute-start | bytes 1572872 | tf_op jit(solution)/shard_map/ppermute | solution.py:559
  103.7 22.8 %collective-permute-start.22 = (bf16[16,128,128]{2,1,0:T(8,128)(2,1)S(1)}, bf16[16,128,128]{2,1,0:T(8,128)(2,1)S(1)}, u32[]{:S(2)}, u32[]{:S(2)}) collective-permute-start(bf16[16,128,128]{2,1,0:T(8,128)(2,1)S(1)} %collective-permute-done.21.mine_ref), channel_id=1, source_target_pairs={{0,8},{24,16},{1,9},{25,17},{2,10},{26,18},{3,11},{27,19},{4,12},{... | collective-permute-start | bytes 1572872 | tf_op jit(solution)/shard_map/ppermute | solution.py:521
  108.1 1.4 collective-permute-start.23
  108.8 28.8 %collective-permute-start.20 = (bf16[8,128,128]{2,1,0:T(8,128)(2,1)S(1)}, bf16[8,128,128]{2,1,0:T(8,128)(2,1)S(1)}, u32[]{:S(2)}, u32[]{:S(2)}) collective-permute-start(bf16[8,128,128]{2,1,0:T(8,128)(2,1)S(1)} %merge.11.refs_2_.after_ref.mine_ref), channel_id=1, source_target_pairs={{8,16},{16,8},{9,17},{17,9},{10,18},{18,10},{11,19},{19,11},{12,20... | collective-permute-start | bytes 786440 | tf_op jit(solution)/shard_map/ppermute | solution.py:544
  120.8 31.0 %collective-permute-start.30 = (bf16[16,128,128]{2,1,0:T(8,128)(2,1)S(1)}, bf16[16,128,128]{2,1,0:T(8,128)(2,1)S(1)}, u32[]{:S(2)}, u32[]{:S(2)}) collective-permute-start(bf16[16,128,128]{2,1,0:T(8,128)(2,1)S(1)} %collective-permute-done.29.mine_ref), channel_id=1, source_target_pairs={{0,8},{24,16},{1,9},{25,17},{2,10},{26,18},{3,11},{27,19},{4,12},{... | collective-permute-start | bytes 1572872 | tf_op jit(solution)/shard_map/ppermute | solution.py:521
  125.2 33.0 %collective-permute-start.19 = (bf16[16,128,128]{2,1,0:T(8,128)(2,1)S(1)}, bf16[16,128,128]{2,1,0:T(8,128)(2,1)S(1)}, u32[]{:S(2)}, u32[]{:S(2)}) collective-permute-start(bf16[16,128,128]{2,1,0:T(8,128)(2,1)S(1)} %collective-permute-done.18.mine_ref), channel_id=1, source_target_pairs={{0,8},{24,16},{1,9},{25,17},{2,10},{26,18},{3,11},{27,19},{4,12},{... | collective-permute-start | bytes 1572872 | tf_op jit(solution)/shard_map/ppermute | solution.py:521
  126.7 25.9 %collective-permute-start.28 = (bf16[16,128,128]{2,1,0:T(8,128)(2,1)S(1)}, bf16[16,128,128]{2,1,0:T(8,128)(2,1)}, u32[]{:S(2)}, u32[]{:S(2)}) collective-permute-start(bf16[16,128,128]{2,1,0:T(8,128)(2,1)S(1)} %merge.13.after_ref.mine_ref), channel_id=1, source_target_pairs={{8,16},{16,8},{9,17},{17,9},{10,18},{18,10},{11,19},{19,11},{12,20... | collective-permute-start | bytes 1572872 | tf_op jit(solution)/shard_map/ppermute | solution.py:544
  128.9 6.1 %collective-permute-start.26 = (f32[64,128]{1,0:T(8,128)S(1)}, f32[64,128]{1,0:T(8,128)S(1)}, u32[]{:S(2)}, u32[]{:S(2)}) collective-permute-start(f32[64,128]{1,0:T(8,128)S(1)} %get-tuple-element.51), channel_id=1, source_target_pairs={{0,1},{1,2},{2,3},{3,4},{4,5},{5,6},{6,7},{8,9},{9,10},{10,11},{11... | collective-permute-start | bytes 98312 | tf_op jit(solution)/shard_map/ppermute | solution.py:553
  135.0 0.6 copy-start.9
  135.7 3.5 %collective-permute-start.27 = (f32[64,128]{1,0:T(8,128)S(1)}, f32[64,128]{1,0:T(8,128)S(1)}, u32[]{:S(2)}, u32[]{:S(2)}) collective-permute-start(f32[64,128]{1,0:T(8,128)S(1)} %get-tuple-element.50), channel_id=1, source_target_pairs={{1,0},{2,1},{3,2},{4,3},{5,4},{6,5},{7,6},{9,8},{10,9},{11,10},{12... | collective-permute-start | bytes 98312 | tf_op jit(solution)/shard_map/ppermute | solution.py:554
  137.6 11.1 %collective-permute-start.25 = (bf16[8,128,128]{2,1,0:T(8,128)(2,1)S(1)}, bf16[8,128,128]{2,1,0:T(8,128)(2,1)}, u32[]{:S(2)}, u32[]{:S(2)}) collective-permute-start(bf16[8,128,128]{2,1,0:T(8,128)(2,1)S(1)} %merge.12.after_ref.refs_5_), channel_id=1, source_target_pairs={{8,0},{16,24},{9,1},{17,25},{10,2},{18,26},{11,3},{19,27},{12,4},{... | collective-permute-start | bytes 786440 | tf_op jit(solution)/shard_map/ppermute | solution.py:544
  139.2 0.6 copy-start.11
  139.8 15.3 %collective-permute-start.24 = (bf16[8,128,128]{2,1,0:T(8,128)(2,1)S(1)}, bf16[8,128,128]{2,1,0:T(8,128)(2,1)}, u32[]{:S(2)}, u32[]{:S(2)}) collective-permute-start(bf16[8,128,128]{2,1,0:T(8,128)(2,1)S(1)} %merge.14.refs_7_.refs_5_), channel_id=1, source_target_pairs={{8,0},{16,24},{9,1},{17,25},{10,2},{18,26},{11,3},{19,27},{12,4},{... | collective-permute-start | bytes 786440 | tf_op jit(solution)/shard_map/ppermute | solution.py:544
  141.1 2.2 %copy-start = (f32[8192,128]{1,0:T(8,128)S(1)}, f32[8192,128]{1,0:T(8,128)}, u32[]{:S(2)}) copy-start(f32[8192,128]{1,0:T(8,128)} %model_ref.3) | copy-start | bytes 12582916
  143.3 0.9 copy-start.8
  144.2 0.8 copy-start.10
  144.9 0.8 copy-start.12
  145.7 3.0 %copy-start.3 = (bf16[128,256]{1,0:T(8,128)(2,1)S(1)}, bf16[128,256]{1,0:T(8,128)(2,1)}, u32[]{:S(2)}) copy-start(bf16[128,256]{1,0:T(8,128)(2,1)} %constant.19.clone.refs_3_) | copy-start | bytes 196612
  145.7 3.0 %copy-start.13 = (s32[1,64]{1,0:T(1,128)S(1)}, s32[1,64]{1,0:T(1,128)}, u32[]{:S(2)}) copy-start(s32[1,64]{1,0:T(1,128)} %refs_2_.9) | copy-start | bytes 772
  151.9 7.1 %collective-permute-start.33 = (bf16[16,128,128]{2,1,0:T(8,128)(2,1)S(1)}, bf16[16,128,128]{2,1,0:T(8,128)(2,1)S(1)}, u32[]{:S(2)}, u32[]{:S(2)}) collective-permute-start(bf16[16,128,128]{2,1,0:T(8,128)(2,1)S(1)} %merge.15.after_ref.mine_ref), channel_id=1, source_target_pairs={{8,16},{16,8},{9,17},{17,9},{10,18},{18,10},{11,19},{19,11},{12,20... | collective-permute-start | bytes 1572872 | tf_op jit(solution)/shard_map/ppermute | solution.py:544
  153.8 17.1 %collective-permute-start.32 = (bf16[16,128,128]{2,1,0:T(8,128)(2,1)S(1)}, bf16[16,128,128]{2,1,0:T(8,128)(2,1)S(1)}, u32[]{:S(2)}, u32[]{:S(2)}) collective-permute-start(bf16[16,128,128]{2,1,0:T(8,128)(2,1)S(1)} %merge.16.refs_7_.refs_5_), channel_id=1, source_target_pairs={{8,0},{16,24},{9,1},{17,25},{10,2},{18,26},{11,3},{19,27},{12,4},{... | collective-permute-start | bytes 1572872 | tf_op jit(solution)/shard_map/ppermute | solution.py:544
  158.3 16.0 %collective-permute-start.31 = (bf16[16,128,128]{2,1,0:T(8,128)(2,1)S(1)}, bf16[16,128,128]{2,1,0:T(8,128)(2,1)S(1)}, u32[]{:S(2)}, u32[]{:S(2)}) collective-permute-start(bf16[16,128,128]{2,1,0:T(8,128)(2,1)S(1)} %merge.17.after_ref.mine_ref), channel_id=1, source_target_pairs={{8,16},{16,8},{9,17},{17,9},{10,18},{18,10},{11,19},{19,11},{12,20... | collective-permute-start | bytes 1572872 | tf_op jit(solution)/shard_map/ppermute | solution.py:544
  159.2 16.5 %copy-start.16 = (bf16[32,128,128]{2,1,0:T(8,128)(2,1)S(1)}, bf16[32,128,128]{2,1,0:T(8,128)(2,1)}, u32[]{:S(2)}) copy-start(bf16[32,128,128]{2,1,0:T(8,128)(2,1)} %get-tuple-element.32) | copy-start | bytes 3145732
  159.2 24.1 %collective-permute-start.35 = (bf16[16,128,128]{2,1,0:T(8,128)(2,1)S(1)}, bf16[16,128,128]{2,1,0:T(8,128)(2,1)S(1)}, u32[]{:S(2)}, u32[]{:S(2)}) collective-permute-start(bf16[16,128,128]{2,1,0:T(8,128)(2,1)S(1)} %merge.18.refs_7_.refs_5_), channel_id=1, source_target_pairs={{8,0},{16,24},{9,1},{17,25},{10,2},{18,26},{11,3},{19,27},{12,4},{... | collective-permute-start | bytes 1572872 | tf_op jit(solution)/shard_map/ppermute | solution.py:544
  174.4 20.0 %collective-permute-start.34 = (bf16[16,128,128]{2,1,0:T(8,128)(2,1)S(1)}, bf16[16,128,128]{2,1,0:T(8,128)(2,1)S(1)}, u32[]{:S(2)}, u32[]{:S(2)}) collective-permute-start(bf16[16,128,128]{2,1,0:T(8,128)(2,1)S(1)} %merge.19.refs_7_.refs_5_), channel_id=1, source_target_pairs={{8,0},{16,24},{9,1},{17,25},{10,2},{18,26},{11,3},{19,27},{12,4},{... | collective-permute-start | bytes 1572872 | tf_op jit(solution)/shard_map/ppermute | solution.py:544
where the time goes:
time: 200 us; the launch traced here: 198 us
  waiting for transfers between devices  71.7 us (36%)
  starting transfers between devices  60.8 us (30%)
  Pallas kernels  49.7 us (25%)
  local copies, waits for them, and re-layouts  11.2 us (6%)
  other arithmetic  3.06 us (2%)
    ppermute x19, waiting for transfers between devices, swap(): lax.ppermute(piece, axis, [(c, c ^ offset) for c in range(lax.axis_size(a...  36.3 us
    ppermute x19, starting transfers between devices, swap(): lax.ppermute(piece, axis, [(c, c ^ offset) for c in range(lax.axis_size(a...  31.4 us
    ppermute x10, waiting for transfers between devices, line_sums(): got[k] = lax.ppermute(state[k], axis, stages[s + 1][0])  25.7 us
    pallas_call x5, Pallas kernels, finish(): pl.pallas_call(lambda *refs: finish_body(*refs, offsets=offsets), out_sha...  16.8 us
    ppermute x5, starting transfers between devices, add_part(): got.append(lax.ppermute(state[-1], axis, stages[0][0]))  14.8 us
    pallas_call x1, Pallas kernels, smoothing(): pl.pallas_call(smooth_body, out_shape=jax.ShapeDtypeStruct((cells, width)...  13.3 us
    ppermute x10, starting transfers between devices, line_sums(): got[k] = lax.ppermute(state[k], axis, stages[s + 1][0])  10.8 us
    unnamed x48, local copies, waits for them, and re-layouts  10.3 us
  transfers between devices with their start and end apart: 36, of which 18 were waited for; matrix products, arithmetic and copies ran while one was open for 1% of the time, Pallas kernels for 15%

commit v1 on v0

--- a/solution.py
+++ b/solution.py
@@ -56,7 +56,7 @@
     if offset % 2:
         target = odd_ref.at[pl.ds((offset // 2) * each, each)]
     else:
-        target = even_refs[offset // 2]
+        target = even_refs[offset // 2].at[pl.ds(0, each)]
     return pltpu.make_async_copy(source, target, sems.at[offset])
 
 
@@ -142,7 +142,7 @@
     )(me, order, model_blocks)
 
 
-def slot_loop(count, sens_ref, block_ref, sems, others, work):
+def slot_loop(count, sens_ref, block_ref, sems, others, acc_ref, work):
     steps = sems.shape[0]
     each = sens_ref.shape[0] // steps
 
@@ -157,6 +157,7 @@
     def _(step):
         block_copy(step).start()
 
+    acc_ref[...] = jnp.zeros_like(acc_ref)
     wait_all(others)
 
     @pl.loop(0, needed)
@@ -174,8 +175,6 @@
     row_blocks = acc_ref.shape[0] - 1
     each = row_blocks // peers
     me = me_ref[0]
-    acc_ref[...] = jnp.zeros_like(acc_ref)
-
     def work(slot, block, live):
         row = jnp.where(live, rows_ref[0, slot], row_blocks)
         acc_ref[row] += jnp.dot(
@@ -183,7 +182,7 @@
         )
 
     waves = gather_pieces([(ref, 0) for ref in wave_refs], held_ref, me, got)
-    slot_loop(count_ref[0, 0], sens_ref, block_ref, sems, waves, work)
+    slot_loop(count_ref[0, 0], sens_ref, block_ref, sems, waves, acc_ref, work)
     stores = []
     for offset in [*range(1, peers, 2), *range(0, peers, 2)]:
         target = odd_ref if offset % 2 else even_ref
@@ -233,8 +232,6 @@
     col_blocks = acc_ref.shape[0] - 1
     each = col_blocks // peers
     me = me_ref[0]
-    acc_ref[...] = jnp.zeros_like(acc_ref)
-
     def work(slot, block, live):
         col = jnp.where(live, cols_ref[0, slot], col_blocks)
         acc_ref[col] += lax.dot_general(
@@ -244,7 +241,7 @@
 
     sources = [(odd_in_ref if o % 2 else even_in_ref, o // 2) for o in range(peers)]
     images = gather_pieces(sources, held_ref, me, got)
-    slot_loop(count_ref[0, 0], sens_ref, block_ref, sems, images, work)
+    slot_loop(count_ref[0, 0], sens_ref, block_ref, sems, images, acc_ref, work)
     stores = []
     for offset in [0, *range(1, peers, 2), *range(2, peers, 2)]:
         part = acc_ref[pl.ds((me ^ offset) * each, each)]
@@ -263,7 +260,9 @@
     image = (RB_DEV, BLK, width)
     outs = pl.pallas_call(
         adjoint_body,
-        out_shape=piece_shapes(piece, peers, jnp.bfloat16)
+        out_shape=[jax.ShapeDtypeStruct(piece, jnp.bfloat16)]
+        + [jax.ShapeDtypeStruct((2 * piece[0], *piece[1:]), jnp.bfloat16)] * (peers // 2 - 1)
+        + piece_shapes(piece, peers, jnp.bfloat16)[-1:]
         + [jax.ShapeDtypeStruct(image, jnp.bfloat16)],
         in_specs=[SMEM_SPEC] * 4 + [ANY_SPEC] * 4,
         out_specs=[ANY_SPEC] * (peers // 2 + 2),
@@ -287,25 +286,35 @@
     return outs[:-2], outs[-2], outs[-1]
 
 
-def join_body(own_ref, other_ref, after_ref, out_ref, *, place):
-    each = own_ref.shape[0]
-    out_ref[:each] = own_ref[...]
-    out_ref[each:] = other_ref[place * each : (place + 1) * each]
-
-
-def join(own, other, place, after):
-    each = own.shape[0]
+def join_body(*refs):
+    count = (len(refs) - 3) // 2
+    other_ref, out_refs, sems = refs[count], refs[count + 2 : -1], refs[-1]
+    each = out_refs[0].shape[0] // 2
+    copies = [
+        pltpu.make_async_copy(
+            other_ref.at[pl.ds((i + 1) * each, each)], out_ref.at[pl.ds(each, each)], sems.at[i]
+        )
+        for i, out_ref in enumerate(out_refs)
+    ]
+    start_all(copies)
+    wait_all(copies)
+
+
+def join(own, other, after):
+    count = len(own)
     return pl.pallas_call(
-        lambda *refs: join_body(*refs, place=place),
-        out_shape=jax.ShapeDtypeStruct((2 * each, *own.shape[1:]), own.dtype),
-        in_specs=[VMEM_SPEC, VMEM_SPEC, ANY_SPEC],
-        out_specs=VMEM_SPEC,
+        join_body,
+        out_shape=[jax.ShapeDtypeStruct(x.shape, x.dtype) for x in own],
+        in_specs=[ANY_SPEC] * (count + 2),
+        out_specs=[ANY_SPEC] * count,
+        input_output_aliases={i: i for i in range(count)},
+        scratch_shapes=[pltpu.SemaphoreType.DMA((count,))],
         compiler_params=pltpu.CompilerParams(vmem_limit_bytes=SMALL),
         cost_estimate=pl.CostEstimate(
-            flops=0, bytes_accessed=8 * own.size, transcendentals=0
+            flops=0, bytes_accessed=4 * other.size, transcendentals=0
         ),
         name="join",
-    )(own, other, after)
+    )(*own, other, after)
 
 
 def tile_value(near, face, window):
@@ -513,15 +522,8 @@
     for hop in range(half - 1):
         left, right = half - 1 - hop, half + hop
         stages.append(([(left, left - 1), (right, right + 1)], True))
-    state, got = [], []
-
-    def add_part(after):
-        if len(state) < count_parts:
-            state.append(make(len(state), after))
-            got.append(lax.ppermute(state[-1], axis, stages[0][0]))
-
-    for _ in range(3):
-        add_part(None)
+    state = [make(k, None) for k in range(2)]
+    got = [lax.ppermute(part, axis, stages[0][0]) for part in state]
     after = state[0]
     for time in range(count_parts + len(stages) - 1):
         for s, (pairs, outwards) in enumerate(stages):
@@ -542,8 +544,10 @@
                     after = deliver(k, jnp.zeros((1,), jnp.int32), state[k], state[k], after)
             if not last:
                 got[k] = lax.ppermute(state[k], axis, stages[s + 1][0])
-            if s == 0:
-                add_part(after)
+            if s == 0 and k == 0:
+                for later in range(2, count_parts):
+                    state.append(make(later, after))
+                    got.append(lax.ppermute(state[-1], axis, stages[0][0]))
 
 
 def halo(block, axis, width):
@@ -595,6 +599,9 @@
         [image_share] + [swap(image_share, "cols", 2 * j) for j in evens], axis=0
     )
     odd_image = swap(even_image, "cols", 1)
+    model_late, _ = lax.optimization_barrier((model_dir, to_send))
+    low, high = halo(model_late, "cols", RIM)
+    smooth = edges(offset, low, model_dir, high, neighbors, face_weight, smooth, to_send)
 
     own, odd, image = adjoint(
         me, blk_row, blk_col, blk_count, sens, even_image, odd_image, smooth, blocks, peers
@@ -603,18 +610,17 @@
     partner = swap(odd, "cols", 1)
     groups = [[0], [1]] + [[2 * j, 2 * j + 1] for j in evens]
 
+    joined = []
+
     def make(chunk, after):
         if chunk == 0:
             return own[0]
         if chunk == 1:
             return partner[:per_peer]
-        j = chunk - 1
-        both = join(own[j], partner, j, own[0] if after is None else after)
-        return swap(both, "cols", 2 * j)
-
-    model_late, _ = lax.optimization_barrier((model_dir, own[0]))
-    low, high = halo(model_late, "cols", RIM)
-    smooth = edges(offset, low, model_dir, high, neighbors, face_weight, smooth, own[0])
+        if not joined:
+            joined.extend(join(own[1:], partner, after))
+        return swap(joined[chunk - 2], "cols", 2 * (chunk - 1))
+
     normal = smooth.reshape(blocks, BLK, width)
 
     def deliver(chunk, take, got, mine, after):

time: 200 us -> 207 us (1.035)
  the two profiles are of different devices: /device:TPU:4 before, /device:TPU:0 now
where the time goes in v1:
time: 207 us; the launch traced here: 205 us
  waiting for transfers between devices  79.6 us (38%)
  starting transfers between devices  60.6 us (29%)
  Pallas kernels  54.4 us (26%)
  local copies, waits for them, and re-layouts  5.51 us (3%)
  other arithmetic  3.06 us (1%)
    ppermute x19, starting transfers between devices, swap(): lax.ppermute(piece, axis, [(c, c ^ offset) for c in range(lax.axis_size(a...  29.8 us
    ppermute x19, waiting for transfers between devices, swap(): lax.ppermute(piece, axis, [(c, c ^ offset) for c in range(lax.axis_size(a...  29.2 us
    ppermute x10, waiting for transfers between devices, line_sums(): got[k] = lax.ppermute(state[k], axis, stages[s + 1][0])  28.1 us
    ppermute x2, waiting for transfers between devices, line_sums(): got = [lax.ppermute(part, axis, stages[0][0]) for part in state]  19.7 us
    pallas_call x5, Pallas kernels, finish(): pl.pallas_call(lambda *refs: finish_body(*refs, offsets=offsets), out_sha...  16.3 us
    ppermute x3, starting transfers between devices, line_sums(): got.append(lax.ppermute(state[-1], axis, stages[0][0]))  13.7 us
    pallas_call x1, Pallas kernels, smoothing(): pl.pallas_call(smooth_body, out_shape=jax.ShapeDtypeStruct((cells, width)...  13.3 us
    ppermute x10, starting transfers between devices, line_sums(): got[k] = lax.ppermute(state[k], axis, stages[s + 1][0])  10.8 us
  transfers between devices with their start and end apart: 36, of which 17 were waited for; matrix products, arithmetic and copies ran while one was open for 1% of the time, Pallas kernels for 14%

profile of v1, /device:TPU:0, one launch (start us, length us, event | category | flops | bytes accessed | tf_op | source)
XLA Modules:
  0.0 205.2 jit_solution(4790330706958374661)
XLA Ops:
  0.6 5.0 %analyze.1 = (bf16[8,128,128]{2,1,0:T(8,128)(2,1)}, bf16[8,128,128]{2,1,0:T(8,128)(2,1)}, bf16[8,128,128]{2,1,0:T(8,128)(2,1)}, bf16[8,128,128]{2,1,0:T(8,128)(2,1)}, bf16[32,128,128]{2,1,0:T(8,128)(2,1)}) custom-call(s32[1]{0:T(128)} %bitcast.me_ref.refs_0_, s32[1,64]{1,0:T(1,128)} %refs_2_.9, f32[64,128,128]{2,1,0:T(8,128)} %bitcast.11), custom_call_target="tpu_custom_call" | custom-call | flops 536870912 | bytes 6291456 | tf_op jit(solution)/shard_map/analyze/pallas_call | solution.py:125
  6.1 2.6 %collective-permute-start.1 = (bf16[8,128,128]{2,1,0:T(8,128)(2,1)}, bf16[8,128,128]{2,1,0:T(8,128)(2,1)S(1)}, u32[]{:S(2)}, u32[]{:S(2)}) collective-permute-start(bf16[8,128,128]{2,1,0:T(8,128)(2,1)} %get-tuple-element.30), channel_id=1, source_target_pairs={{0,2},{1,3},{2,0},{3,1},{4,6},{5,7},{6,4},{7,5},{8,10},{9,11},{10,... | collective-permute-start | bytes 786440 | tf_op jit(solution)/shard_map/ppermute | solution.py:563
  8.7 1.5 collective-permute-start.3
  11.0 2.0 collective-permute-start.2
  13.0 1.5 collective-permute-start.4
  14.5 1.6 collective-permute-done.1.refs_2_
  16.0 2.9 %collective-permute-start.6 = (bf16[8,128,128]{2,1,0:T(8,128)(2,1)S(1)}, bf16[8,128,128]{2,1,0:T(8,128)(2,1)S(1)}, u32[]{:S(2)}, u32[]{:S(2)}) collective-permute-start(bf16[8,128,128]{2,1,0:T(8,128)(2,1)S(1)} %get-tuple-element.58), channel_id=1, source_target_pairs={{0,6},{1,7},{2,4},{3,5},{4,2},{5,3},{6,0},{7,1},{8,14},{9,15},{10,... | collective-permute-start | bytes 786440 | tf_op jit(solution)/shard_map/ppermute | solution.py:563
  19.0 13.3 %smoothing.1.refs_8_.base_ref = f32[8192,128]{1,0:T(8,128)} custom-call(s32[1]{0:T(128)} %bitcast.3.offset_ref, f32[8192,128]{1,0:T(8,128)} %model_ref.3, s32[4,8192]{1,0:T(4,128)} %near_ref.3, f32[4,8192]{1,0:T(4,128)} %weight_ref.3, bf16[32,128,128]{2,1,0:T(8,128)(2,1)} %copy-done.9), custom_call_target="tpu_custom_call" | custom-call | flops 3221225472 | bytes 16777216 | tf_op jit(solution)/shard_map/smoothing/pallas_call | solution.py:374
  32.3 1.8 collective-permute-done.4.refs_5_
  34.9 7.5 %forward.1 = (f32[16,128,128]{2,1,0:T(8,128)}, f32[16,128,128]{2,1,0:T(8,128)}) custom-call(s32[1]{0:T(128)} %bitcast.me_ref.refs_0_, s32[1,384]{1,0:T(1,128)} %rows_ref.3, s32[1,384]{1,0:T(1,128)} %cols_ref.3, s32[1,1]{1,0:T(1,128)S(6)} %copy.33.count_ref, bf16[384,128,128]{2,1,0:T(8,128)(2,1)} %bitcast.15, bf16[8,128,128]{2,1,0:T(8,128)(2,1)} %get-tuple-element.28.refs_0_, ...), custom_call_target="tpu_custom_call" | custom-call | flops 1610612736 | bytes 12582912 | tf_op jit(solution)/shard_map/forward/pallas_call | solution.py:205
  42.5 3.5 %collective-permute-start.7 = (f32[16,128,128]{2,1,0:T(8,128)}, f32[16,128,128]{2,1,0:T(8,128)S(1)}, u32[]{:S(2)}, u32[]{:S(2)}) collective-permute-start(f32[16,128,128]{2,1,0:T(8,128)} %get-tuple-element.34), channel_id=1, source_target_pairs={{0,1},{1,0},{2,3},{3,2},{4,5},{5,4},{6,7},{7,6},{8,9},{9,8},{10,11... | collective-permute-start | bytes 3145736 | tf_op jit(solution)/shard_map/ppermute | solution.py:563
  46.0 2.5 %collective-permute-done.7 = f32[16,128,128]{2,1,0:T(8,128)S(1)} collective-permute-done((f32[16,128,128]{2,1,0:T(8,128)}, f32[16,128,128]{2,1,0:T(8,128)S(1)}, u32[]{:S(2)}, u32[]{:S(2)}) %collective-permute-start.7) | collective-permute-done | bytes 1048608 | tf_op jit(solution)/shard_map/ppermute | solution.py:563
  48.5 1.4 fusion.1
  49.9 1.6 collective-permute-start.10
  51.5 2.0 collective-permute-start.9
  53.5 3.8 %collective-permute-done.10 = bf16[4,128,128]{2,1,0:T(8,128)(2,1)S(1)} collective-permute-done((bf16[4,128,128]{2,1,0:T(8,128)(2,1)S(1)}, bf16[4,128,128]{2,1,0:T(8,128)(2,1)S(1)}, u32[]{:S(2)}, u32[]{:S(2)}) %collective-permute-start.10) | collective-permute-done | bytes 131104 | tf_op jit(solution)/shard_map/ppermute | solution.py:563
  57.5 2.0 collective-permute-done.9
  60.0 1.5 collective-permute-start.12
  61.5 1.7 collective-permute-start.13
  63.1 2.9 %collective-permute-done.11 = bf16[4,128,128]{2,1,0:T(8,128)(2,1)S(1)} collective-permute-done((bf16[4,128,128]{2,1,0:T(8,128)(2,1)S(1)}, bf16[4,128,128]{2,1,0:T(8,128)(2,1)S(1)}, u32[]{:S(2)}, u32[]{:S(2)}) %collective-permute-start.11) | collective-permute-done | bytes 131104 | tf_op jit(solution)/shard_map/ppermute | solution.py:563
  66.0 2.0 collective-permute-done.12
  68.1 2.4 %collective-permute-start.15 = (f32[64,128]{1,0:T(8,128)S(1)}, f32[64,128]{1,0:T(8,128)S(1)}, u32[]{:S(2)}, u32[]{:S(2)}) collective-permute-start(f32[64,128]{1,0:T(8,128)S(1)} %get-tuple-element.57), channel_id=1, source_target_pairs={{0,1},{1,2},{2,3},{3,4},{4,5},{5,6},{6,7},{8,9},{9,10},{10,11},{11... | collective-permute-start | bytes 98312 | tf_op jit(solution)/shard_map/ppermute | solution.py:557
  70.5 1.3 collective-permute-start.16
  71.8 2.6 %collective-permute-done.16.high_ref = f32[64,128]{1,0:T(8,128)S(1)} collective-permute-done((f32[64,128]{1,0:T(8,128)S(1)}, f32[64,128]{1,0:T(8,128)S(1)}, u32[]{:S(2)}, u32[]{:S(2)}) %collective-permute-start.16) | collective-permute-done | bytes 32800 | tf_op jit(solution)/shard_map/ppermute | solution.py:558
  74.4 1.4 edges.1.after_ref
  75.9 0.8 copy-done.12
  76.7 8.0 %adjoint.1 = (bf16[8,128,128]{2,1,0:T(8,128)(2,1)}, bf16[16,128,128]{2,1,0:T(8,128)(2,1)}, bf16[16,128,128]{2,1,0:T(8,128)(2,1)}, bf16[16,128,128]{2,1,0:T(8,128...) custom-call(s32[1]{0:T(128)} %bitcast.me_ref.refs_0_, s32[1,384]{1,0:T(1,128)} %rows_ref.3, ...), custom_call_target="tpu_custom_call" | custom-call | flops 1610612736 | bytes 12582912 | tf_op jit(solution)/shard_map/adjoint/pallas_call | solution.py:261
  84.8 7.2 %collective-permute-start.17 = (bf16[32,128,128]{2,1,0:T(8,128)(2,1)}, bf16[32,128,128]{2,1,0:T(8,128)(2,1)S(1)}, u32[]{:S(2)}, u32[]{:S(2)}) collective-permute-start(bf16[32,128,128]{2,1,0:T(8,128)(2,1)} %get-tuple-element.40), channel_id=1, source_target_pairs={{0,1},{1,0},{2,3},{3,2},{4,5},{5,4},{6,7},{7,6},{8,9},{9,8},{10,11... | collective-permute-start | bytes 3145736 | tf_op jit(solution)/shard_map/ppermute | solution.py:563
  92.0 1.3 collective-permute-start.18
  93.3 6.3 %collective-permute-done.18.got_ref = bf16[8,128,128]{2,1,0:T(8,128)(2,1)S(1)} collective-permute-done((bf16[8,128,128]{2,1,0:T(8,128)(2,1)}, bf16[8,128,128]{2,1,0:T(8,128)(2,1)S(1)}, u32[]{:S(2)}, u32[]{:S(2)}) %collective-permute-start.18) | collective-permute-done | bytes 262176 | tf_op jit(solution)/shard_map/ppermute | solution.py:526
  99.6 0.9 copy-done.2
  100.6 1.0 copy-done.3
  101.6 1.0 copy-done.4
  102.7 0.8 join.1
  103.5 0.8 copy-done.5
  104.3 0.8 collective-permute-start.23
  105.0 12.6 %collective-permute-done.23.mine_ref = bf16[16,128,128]{2,1,0:T(8,128)(2,1)S(1)} collective-permute-done((bf16[16,128,128]{2,1,0:T(8,128)(2,1)S(1)}, bf16[16,128,128]{2,1,0:T(8,128)(2,1)S(1)}, u32[]{:S(2)}, u32[]{:S(2)}) %collective-permute-start.23) | collective-permute-done | bytes 524320 | tf_op jit(solution)/shard_map/ppermute | solution.py:563
  117.6 4.3 %collective-permute-start.24 = (bf16[16,128,128]{2,1,0:T(8,128)(2,1)S(1)}, bf16[16,128,128]{2,1,0:T(8,128)(2,1)S(1)}, u32[]{:S(2)}, u32[]{:S(2)}) collective-permute-start(bf16[16,128,128]{2,1,0:T(8,128)(2,1)S(1)} %collective-permute-done.23.mine_ref), channel_id=1, source_target_pairs={{0,8},{24,16},{1,9},{25,17},{2,10},{26,18},{3,11},{27,19},{4,12},{... | collective-permute-start | bytes 1572872 | tf_op jit(solution)/shard_map/ppermute | solution.py:550
  122.0 1.3 collective-permute-start.21
  123.3 0.7 collective-permute-start.25
  124.0 13.4 %collective-permute-done.21.got_ref = bf16[8,128,128]{2,1,0:T(8,128)(2,1)S(1)} collective-permute-done((bf16[8,128,128]{2,1,0:T(8,128)(2,1)S(1)}, bf16[8,128,128]{2,1,0:T(8,128)(2,1)S(1)}, u32[]{:S(2)}, u32[]{:S(2)}) %collective-permute-start.21) | collective-permute-done | bytes 262176 | tf_op jit(solution)/shard_map/ppermute | solution.py:526
  137.5 4.4 %collective-permute-start.30 = (bf16[16,128,128]{2,1,0:T(8,128)(2,1)S(1)}, bf16[16,128,128]{2,1,0:T(8,128)(2,1)S(1)}, u32[]{:S(2)}, u32[]{:S(2)}) collective-permute-start(bf16[16,128,128]{2,1,0:T(8,128)(2,1)S(1)} %collective-permute-done.29.mine_ref), channel_id=1, source_target_pairs={{0,8},{24,16},{1,9},{25,17},{2,10},{26,18},{3,11},{27,19},{4,12},{... | collective-permute-start | bytes 1572872 | tf_op jit(solution)/shard_map/ppermute | solution.py:550
  142.1 1.5 collective-permute-start.28
  143.6 0.7 collective-permute-start.22
  144.3 5.0 %collective-permute-start.20 = (bf16[16,128,128]{2,1,0:T(8,128)(2,1)S(1)}, bf16[16,128,128]{2,1,0:T(8,128)(2,1)S(1)}, u32[]{:S(2)}, u32[]{:S(2)}) collective-permute-start(bf16[16,128,128]{2,1,0:T(8,128)(2,1)S(1)} %collective-permute-done.19.mine_ref), channel_id=1, source_target_pairs={{0,8},{24,16},{1,9},{25,17},{2,10},{26,18},{3,11},{27,19},{4,12},{... | collective-permute-start | bytes 1572872 | tf_op jit(solution)/shard_map/ppermute | solution.py:550
  149.3 1.3 collective-permute-start.27
  150.7 1.3 collective-permute-start.26
  152.0 5.7 %collective-permute-done.27.refs_4_ = bf16[8,128,128]{2,1,0:T(8,128)(2,1)} collective-permute-done((bf16[8,128,128]{2,1,0:T(8,128)(2,1)S(1)}, bf16[8,128,128]{2,1,0:T(8,128)(2,1)}, u32[]{:S(2)}, u32[]{:S(2)}) %collective-permute-start.27) | collective-permute-done | bytes 262176 | tf_op jit(solution)/shard_map/ppermute | solution.py:546
  157.7 3.1 %finish.5 = (f32[64,128,128]{2,1,0:T(8,128)}, f32[8,128]{1,0:T(8,128)S(1)}) custom-call(s32[1]{0:T(128)} %bitcast.me_ref.refs_0_, s32[1]{0:T(128)} %bitcast.6.refs_1_, s32[1,64]{1,0:T(1,128)S(1)} %copy-done.8, bf16[128,256]{1,0:T(8,128)(2,1)S(1)} %copy-done.1, bf16[8,128,128]{2,1,0:T(8,128)(2,1)} %collective-permute-done.27.refs_4_, ...), custom_call_target="tpu_custom_call", output_to_operand_aliasing={{0}: (6, {})} | custom-call | flops 67108864 | bytes 1310720 | tf_op jit(solution)/shard_map/finish/pallas_call | solution.py:471
  160.9 0.7 collective-permute-start.33
  161.6 1.2 merge.16.refs_7_.refs_5_
  162.7 1.3 collective-permute-start.32
  164.0 2.1 %collective-permute-done.26.refs_4_ = bf16[8,128,128]{2,1,0:T(8,128)(2,1)S(1)} collective-permute-done((bf16[8,128,128]{2,1,0:T(8,128)(2,1)S(1)}, bf16[8,128,128]{2,1,0:T(8,128)(2,1)S(1)}, u32[]{:S(2)}, u32[]{:S(2)}) %collective-permute-start.26) | collective-permute-done | bytes 262176 | tf_op jit(solution)/shard_map/ppermute | solution.py:546
  166.1 2.6 %finish.6 = (f32[64,128,128]{2,1,0:T(8,128)}, f32[8,128]{1,0:T(8,128)S(1)}) custom-call(s32[1]{0:T(128)} %bitcast.me_ref.refs_0_, s32[1]{0:T(128)} %bitcast.6.refs_1_, s32[1,64]{1,0:T(1,128)S(1)} %copy-done.8, bf16[128,256]{1,0:T(8,128)(2,1)S(1)} %copy-done.1, ...), custom_call_target="tpu_custom_call", output_to_operand_aliasing={{0}: (6, {})} | custom-call | flops 67108864 | bytes 1310720 | tf_op jit(solution)/shard_map/finish/pallas_call | solution.py:471
  168.9 0.7 collective-permute-start.31
  169.8 1.4 collective-permute-start.35
  171.2 10.1 %collective-permute-done.32.refs_4_ = bf16[16,128,128]{2,1,0:T(8,128)(2,1)S(1)} collective-permute-done((bf16[16,128,128]{2,1,0:T(8,128)(2,1)S(1)}, bf16[16,128,128]{2,1,0:T(8,128)(2,1)S(1)}, u32[]{:S(2)}, u32[]{:S(2)}) %collective-permute-start.32) | collective-permute-done | bytes 524320 | tf_op jit(solution)/shard_map/ppermute | solution.py:546
  181.3 3.4 %finish.7 = (f32[64,128,128]{2,1,0:T(8,128)}, f32[8,128]{1,0:T(8,128)S(1)}) custom-call(s32[1]{0:T(128)} %bitcast.me_ref.refs_0_, s32[1]{0:T(128)} %bitcast.6.refs_1_, s32[1,64]{1,0:T(1,128)S(1)} %copy-done.8, bf16[128,256]{1,0:T(8,128)(2,1)S(1)} %copy-done.1, ...), custom_call_target="tpu_custom_call", output_to_operand_aliasing={{0}: (6, {})} | custom-call | flops 134217728 | bytes 2621440 | tf_op jit(solution)/shard_map/finish/pallas_call | solution.py:471
  184.8 1.3 collective-permute-start.34
  186.1 1.5 bitcast_convert_fusion
  187.7 4.7 %collective-permute-done.35.refs_4_ = bf16[16,128,128]{2,1,0:T(8,128)(2,1)S(1)} collective-permute-done((bf16[16,128,128]{2,1,0:T(8,128)(2,1)S(1)}, bf16[16,128,128]{2,1,0:T(8,128)(2,1)S(1)}, u32[]{:S(2)}, u32[]{:S(2)}) %collective-permute-start.35) | collective-permute-done | bytes 524320 | tf_op jit(solution)/shard_map/ppermute | solution.py:546
  192.3 3.4 %finish.8 = (f32[64,128,128]{2,1,0:T(8,128)}, f32[8,128]{1,0:T(8,128)S(1)}) custom-call(s32[1]{0:T(128)} %bitcast.me_ref.refs_0_, s32[1]{0:T(128)} %bitcast.6.refs_1_, s32[1,64]{1,0:T(1,128)S(1)} %copy-done.8, bf16[128,256]{1,0:T(8,128)(2,1)S(1)} %copy-done.1, ...), custom_call_target="tpu_custom_call", output_to_operand_aliasing={{0}: (6, {})} | custom-call | flops 134217728 | bytes 2621440 | tf_op jit(solution)/shard_map/finish/pallas_call | solution.py:471
  195.7 5.5 %collective-permute-done.34.refs_4_ = bf16[16,128,128]{2,1,0:T(8,128)(2,1)S(1)} collective-permute-done((bf16[16,128,128]{2,1,0:T(8,128)(2,1)S(1)}, bf16[16,128,128]{2,1,0:T(8,128)(2,1)S(1)}, u32[]{:S(2)}, u32[]{:S(2)}) %collective-permute-start.34) | collective-permute-done | bytes 524320 | tf_op jit(solution)/shard_map/ppermute | solution.py:546
  201.2 3.9 %finish.9 = (f32[64,128,128]{2,1,0:T(8,128)}, f32[8,128]{1,0:T(8,128)}) custom-call(s32[1]{0:T(128)} %bitcast.me_ref.refs_0_, s32[1]{0:T(128)} %bitcast.6.refs_1_, s32[1,64]{1,0:T(1,128)S(1)} %copy-done.8, bf16[128,256]{1,0:T(8,128)(2,1)S(1)} %copy-done.1, ...), custom_call_target="tpu_custom_call", output_to_operand_aliasing={{0}: (6, {})} | custom-call | flops 134217728 | bytes 2621440 | tf_op jit(solution)/shard_map/finish/pallas_call | solution.py:471
  (75 shorter events, 3.3 us)
Async XLA Ops:
  5.6 5.3 %collective-permute-start = (bf16[32,128,128]{2,1,0:T(8,128)(2,1)}, bf16[32,128,128]{2,1,0:T(8,128)(2,1)S(1)}, u32[]{:S(2)}, u32[]{:S(2)}) collective-permute-start(bf16[32,128,128]{2,1,0:T(8,128)(2,1)} %get-tuple-element.29), channel_id=1, source_target_pairs={{0,1},{1,0},{2,3},{3,2},{4,5},{5,4},{6,7},{7,6},{8,9},{9,8},{10,11... | collective-permute-start | bytes 3145736 | tf_op jit(solution)/shard_map/ppermute | solution.py:563
  6.1 9.9 %collective-permute-start.1 = (bf16[8,128,128]{2,1,0:T(8,128)(2,1)}, bf16[8,128,128]{2,1,0:T(8,128)(2,1)S(1)}, u32[]{:S(2)}, u32[]{:S(2)}) collective-permute-start(bf16[8,128,128]{2,1,0:T(8,128)(2,1)} %get-tuple-element.30), channel_id=1, source_target_pairs={{0,2},{1,3},{2,0},{3,1},{4,6},{5,7},{6,4},{7,5},{8,10},{9,11},{10,... | collective-permute-start | bytes 786440 | tf_op jit(solution)/shard_map/ppermute | solution.py:563
  8.7 23.6 %collective-permute-start.3 = (bf16[8,128,128]{2,1,0:T(8,128)(2,1)}, bf16[8,128,128]{2,1,0:T(8,128)(2,1)S(1)}, u32[]{:S(2)}, u32[]{:S(2)}) collective-permute-start(bf16[8,128,128]{2,1,0:T(8,128)(2,1)} %get-tuple-element.31), channel_id=1, source_target_pairs={{0,4},{1,5},{2,6},{3,7},{4,0},{5,1},{6,2},{7,3},{8,12},{9,13},{10,... | collective-permute-start | bytes 786440 | tf_op jit(solution)/shard_map/ppermute | solution.py:563
  10.2 22.1 %collective-permute-start.5 = (bf16[8,128,128]{2,1,0:T(8,128)(2,1)}, bf16[8,128,128]{2,1,0:T(8,128)(2,1)S(1)}, u32[]{:S(2)}, u32[]{:S(2)}) collective-permute-start(bf16[8,128,128]{2,1,0:T(8,128)(2,1)} %get-tuple-element.32), channel_id=1, source_target_pairs={{0,6},{1,7},{2,4},{3,5},{4,2},{5,3},{6,0},{7,1},{8,14},{9,15},{10,... | collective-permute-start | bytes 786440 | tf_op jit(solution)/shard_map/ppermute | solution.py:563
  10.9 8.1 %copy-start.9 = (bf16[32,128,128]{2,1,0:T(8,128)(2,1)}, bf16[32,128,128]{2,1,0:T(8,128)(2,1)S(1)}, u32[]{:S(2)}) copy-start(bf16[32,128,128]{2,1,0:T(8,128)(2,1)S(1)} %collective-permute-done.after_ref.refs_1_) | copy-start | bytes 3145732
  11.0 21.4 %collective-permute-start.2 = (bf16[8,128,128]{2,1,0:T(8,128)(2,1)S(1)}, bf16[8,128,128]{2,1,0:T(8,128)(2,1)S(1)}, u32[]{:S(2)}, u32[]{:S(2)}) collective-permute-start(bf16[8,128,128]{2,1,0:T(8,128)(2,1)S(1)} %get-tuple-element.60), channel_id=1, source_target_pairs={{0,2},{1,3},{2,0},{3,1},{4,6},{5,7},{6,4},{7,5},{8,10},{9,11},{10,... | collective-permute-start | bytes 786440 | tf_op jit(solution)/shard_map/ppermute | solution.py:563
  13.0 21.1 %collective-permute-start.4 = (bf16[8,128,128]{2,1,0:T(8,128)(2,1)S(1)}, bf16[8,128,128]{2,1,0:T(8,128)(2,1)S(1)}, u32[]{:S(2)}, u32[]{:S(2)}) collective-permute-start(bf16[8,128,128]{2,1,0:T(8,128)(2,1)S(1)} %get-tuple-element.59), channel_id=1, source_target_pairs={{0,4},{1,5},{2,6},{3,7},{4,0},{5,1},{6,2},{7,3},{8,12},{9,13},{10,... | collective-permute-start | bytes 786440 | tf_op jit(solution)/shard_map/ppermute | solution.py:563
  16.0 16.2 %copy-start.13 = (bf16[8,128,128]{2,1,0:T(8,128)(2,1)}, bf16[8,128,128]{2,1,0:T(8,128)(2,1)S(1)}, u32[]{:S(2)}) copy-start(bf16[8,128,128]{2,1,0:T(8,128)(2,1)S(1)} %collective-permute-done.1.refs_2_) | copy-start | bytes 786436
  16.0 18.1 %collective-permute-start.6 = (bf16[8,128,128]{2,1,0:T(8,128)(2,1)S(1)}, bf16[8,128,128]{2,1,0:T(8,128)(2,1)S(1)}, u32[]{:S(2)}, u32[]{:S(2)}) collective-permute-start(bf16[8,128,128]{2,1,0:T(8,128)(2,1)S(1)} %get-tuple-element.58), channel_id=1, source_target_pairs={{0,6},{1,7},{2,4},{3,5},{4,2},{5,3},{6,0},{7,1},{8,14},{9,15},{10,... | collective-permute-start | bytes 786440 | tf_op jit(solution)/shard_map/ppermute | solution.py:563
  32.3 1.8 copy-start.14
  32.3 1.8 copy-start.15
  32.3 1.8 copy-start.16
  34.1 0.7 copy-start.17
  34.1 0.8 copy-start.18
  42.4 25.7 %copy-start = (f32[8192,128]{1,0:T(8,128)S(1)}, f32[8192,128]{1,0:T(8,128)}, u32[]{:S(2)}) copy-start(f32[8192,128]{1,0:T(8,128)} %model_ref.3) | copy-start | bytes 12582916
  42.4 32.0 %copy-start.6 = (s32[4,8192]{1,0:T(4,128)S(1)}, s32[4,8192]{1,0:T(4,128)}, u32[]{:S(2)}) copy-start(s32[4,8192]{1,0:T(4,128)} %near_ref.3) | copy-start | bytes 393220
  42.5 32.0 %copy-start.7 = (f32[4,8192]{1,0:T(4,128)S(1)}, f32[4,8192]{1,0:T(4,128)}, u32[]{:S(2)}) copy-start(f32[4,8192]{1,0:T(4,128)} %weight_ref.3) | copy-start | bytes 393220
  42.5 6.0 %collective-permute-start.7 = (f32[16,128,128]{2,1,0:T(8,128)}, f32[16,128,128]{2,1,0:T(8,128)S(1)}, u32[]{:S(2)}, u32[]{:S(2)}) collective-permute-start(f32[16,128,128]{2,1,0:T(8,128)} %get-tuple-element.34), channel_id=1, source_target_pairs={{0,1},{1,0},{2,3},{3,2},{4,5},{5,4},{6,7},{7,6},{8,9},{9,8},{10,11... | collective-permute-start | bytes 3145736 | tf_op jit(solution)/shard_map/ppermute | solution.py:563
  49.9 7.3 %collective-permute-start.10 = (bf16[4,128,128]{2,1,0:T(8,128)(2,1)S(1)}, bf16[4,128,128]{2,1,0:T(8,128)(2,1)S(1)}, u32[]{:S(2)}, u32[]{:S(2)}) collective-permute-start(bf16[4,128,128]{2,1,0:T(8,128)(2,1)S(1)} %get-tuple-element.62), channel_id=1, source_target_pairs={{0,6},{1,7},{2,4},{3,5},{4,2},{5,3},{6,0},{7,1},{8,14},{9,15},{10,... | collective-permute-start | bytes 393224 | tf_op jit(solution)/shard_map/ppermute | solution.py:563
  51.5 5.9 %collective-permute-start.8 = (bf16[4,128,128]{2,1,0:T(8,128)(2,1)S(1)}, bf16[4,128,128]{2,1,0:T(8,128)(2,1)S(1)}, u32[]{:S(2)}, u32[]{:S(2)}) collective-permute-start(bf16[4,128,128]{2,1,0:T(8,128)(2,1)S(1)} %get-tuple-element.61), channel_id=1, source_target_pairs={{0,2},{1,3},{2,0},{3,1},{4,6},{5,7},{6,4},{7,5},{8,10},{9,11},{10,... | collective-permute-start | bytes 393224 | tf_op jit(solution)/shard_map/ppermute | solution.py:563
  51.5 8.0 %collective-permute-start.9 = (bf16[4,128,128]{2,1,0:T(8,128)(2,1)S(1)}, bf16[4,128,128]{2,1,0:T(8,128)(2,1)S(1)}, u32[]{:S(2)}, u32[]{:S(2)}) collective-permute-start(bf16[4,128,128]{2,1,0:T(8,128)(2,1)S(1)} %get-tuple-element.63), channel_id=1, source_target_pairs={{0,4},{1,5},{2,6},{3,7},{4,0},{5,1},{6,2},{7,3},{8,12},{9,13},{10,... | collective-permute-start | bytes 393224 | tf_op jit(solution)/shard_map/ppermute | solution.py:563
  59.6 6.4 %collective-permute-start.11 = (bf16[4,128,128]{2,1,0:T(8,128)(2,1)S(1)}, bf16[4,128,128]{2,1,0:T(8,128)(2,1)S(1)}, u32[]{:S(2)}, u32[]{:S(2)}) collective-permute-start(bf16[4,128,128]{2,1,0:T(8,128)(2,1)S(1)} %fusion), channel_id=1, source_target_pairs={{0,2},{1,3},{2,0},{3,1},{4,6},{5,7},{6,4},{7,5},{8,10},{9,11},{10,... | collective-permute-start | bytes 393224 | tf_op jit(solution)/shard_map/ppermute | solution.py:563
  60.0 7.9 %collective-permute-start.12 = (bf16[4,128,128]{2,1,0:T(8,128)(2,1)S(1)}, bf16[4,128,128]{2,1,0:T(8,128)(2,1)S(1)}, u32[]{:S(2)}, u32[]{:S(2)}) collective-permute-start(bf16[4,128,128]{2,1,0:T(8,128)(2,1)S(1)} %fusion), channel_id=1, source_target_pairs={{0,4},{1,5},{2,6},{3,7},{4,0},{5,1},{6,2},{7,3},{8,12},{9,13},{10,... | collective-permute-start | bytes 393224 | tf_op jit(solution)/shard_map/ppermute | solution.py:563
  61.5 6.5 %collective-permute-start.13 = (bf16[4,128,128]{2,1,0:T(8,128)(2,1)S(1)}, bf16[4,128,128]{2,1,0:T(8,128)(2,1)S(1)}, u32[]{:S(2)}, u32[]{:S(2)}) collective-permute-start(bf16[4,128,128]{2,1,0:T(8,128)(2,1)S(1)} %fusion), channel_id=1, source_target_pairs={{0,6},{1,7},{2,4},{3,5},{4,2},{5,3},{6,0},{7,1},{8,14},{9,15},{10,... | collective-permute-start | bytes 393224 | tf_op jit(solution)/shard_map/ppermute | solution.py:563
  68.0 7.9 %copy-start.10 = (bf16[16,128,128]{2,1,0:T(8,128)(2,1)}, bf16[16,128,128]{2,1,0:T(8,128)(2,1)S(1)}, u32[]{:S(2)}) copy-start(bf16[16,128,128]{2,1,0:T(8,128)(2,1)S(1)} %pad_maximum_fusion.even_in_ref) | copy-start | bytes 1572868
  68.0 7.9 %collective-permute-start.14 = (bf16[16,128,128]{2,1,0:T(8,128)(2,1)S(1)}, bf16[16,128,128]{2,1,0:T(8,128)(2,1)S(1)}, u32[]{:S(2)}, u32[]{:S(2)}) collective-permute-start(bf16[16,128,128]{2,1,0:T(8,128)(2,1)S(1)} %pad_maximum_fusion.even_in_ref), channel_id=1, source_target_pairs={{0,1},{1,0},{2,3},{3,2},{4,5},{5,4},{6,7},{7,6},{8,9},{9,8},{10,11... | collective-permute-start | bytes 1572872 | tf_op jit(solution)/shard_map/ppermute | solution.py:563
  68.1 3.7 %collective-permute-start.15 = (f32[64,128]{1,0:T(8,128)S(1)}, f32[64,128]{1,0:T(8,128)S(1)}, u32[]{:S(2)}, u32[]{:S(2)}) collective-permute-start(f32[64,128]{1,0:T(8,128)S(1)} %get-tuple-element.57), channel_id=1, source_target_pairs={{0,1},{1,2},{2,3},{3,4},{4,5},{5,6},{6,7},{8,9},{9,10},{10,11},{11... | collective-permute-start | bytes 98312 | tf_op jit(solution)/shard_map/ppermute | solution.py:557
  70.5 3.9 %collective-permute-start.16 = (f32[64,128]{1,0:T(8,128)S(1)}, f32[64,128]{1,0:T(8,128)S(1)}, u32[]{:S(2)}, u32[]{:S(2)}) collective-permute-start(f32[64,128]{1,0:T(8,128)S(1)} %get-tuple-element.56), channel_id=1, source_target_pairs={{1,0},{2,1},{3,2},{4,3},{5,4},{6,5},{7,6},{9,8},{10,9},{11,10},{12... | collective-permute-start | bytes 98312 | tf_op jit(solution)/shard_map/ppermute | solution.py:558
  75.9 0.8 copy-start.12
  84.8 15.8 %collective-permute-start.17 = (bf16[32,128,128]{2,1,0:T(8,128)(2,1)}, bf16[32,128,128]{2,1,0:T(8,128)(2,1)S(1)}, u32[]{:S(2)}, u32[]{:S(2)}) collective-permute-start(bf16[32,128,128]{2,1,0:T(8,128)(2,1)} %get-tuple-element.40), channel_id=1, source_target_pairs={{0,1},{1,0},{2,3},{3,2},{4,5},{5,4},{6,7},{7,6},{8,9},{9,8},{10,11... | collective-permute-start | bytes 3145736 | tf_op jit(solution)/shard_map/ppermute | solution.py:563
  92.0 7.6 %collective-permute-start.18 = (bf16[8,128,128]{2,1,0:T(8,128)(2,1)}, bf16[8,128,128]{2,1,0:T(8,128)(2,1)S(1)}, u32[]{:S(2)}, u32[]{:S(2)}) collective-permute-start(bf16[8,128,128]{2,1,0:T(8,128)(2,1)} %get-tuple-element.41.mine_ref.after_ref), channel_id=1, source_target_pairs={{0,8},{24,16},{1,9},{25,17},{2,10},{26,18},{3,11},{27,19},{4,12},{... | collective-permute-start | bytes 786440 | tf_op jit(solution)/shard_map/ppermute | solution.py:526
  99.6 0.9 copy-start.2
  100.6 1.0 copy-start.3
  101.6 1.0 copy-start.4
  102.7 55.0 %copy-start.1 = (bf16[128,256]{1,0:T(8,128)(2,1)S(1)}, bf16[128,256]{1,0:T(8,128)(2,1)}, u32[]{:S(2)}) copy-start(bf16[128,256]{1,0:T(8,128)(2,1)} %constant.19.clone.refs_3_) | copy-start | bytes 196612
  102.7 55.0 %copy-start.8 = (s32[1,64]{1,0:T(1,128)S(1)}, s32[1,64]{1,0:T(1,128)}, u32[]{:S(2)}) copy-start(s32[1,64]{1,0:T(1,128)} %refs_2_.9) | copy-start | bytes 772
  103.5 0.8 copy-start.5
  104.3 13.3 %collective-permute-start.23 = (bf16[16,128,128]{2,1,0:T(8,128)(2,1)S(1)}, bf16[16,128,128]{2,1,0:T(8,128)(2,1)S(1)}, u32[]{:S(2)}, u32[]{:S(2)}) collective-permute-start(bf16[16,128,128]{2,1,0:T(8,128)(2,1)S(1)} %get-tuple-element.43), channel_id=1, source_target_pairs={{0,2},{1,3},{2,0},{3,1},{4,6},{5,7},{6,4},{7,5},{8,10},{9,11},{10,... | collective-permute-start | bytes 1572872 | tf_op jit(solution)/shard_map/ppermute | solution.py:563
  105.0 32.4 %collective-permute-start.29 = (bf16[16,128,128]{2,1,0:T(8,128)(2,1)}, bf16[16,128,128]{2,1,0:T(8,128)(2,1)S(1)}, u32[]{:S(2)}, u32[]{:S(2)}) collective-permute-start(bf16[16,128,128]{2,1,0:T(8,128)(2,1)} %get-tuple-element.45), channel_id=1, source_target_pairs={{0,4},{1,5},{2,6},{3,7},{4,0},{5,1},{6,2},{7,3},{8,12},{9,13},{10,... | collective-permute-start | bytes 1572872 | tf_op jit(solution)/shard_map/ppermute | solution.py:563
  117.6 24.4 %collective-permute-start.24 = (bf16[16,128,128]{2,1,0:T(8,128)(2,1)S(1)}, bf16[16,128,128]{2,1,0:T(8,128)(2,1)S(1)}, u32[]{:S(2)}, u32[]{:S(2)}) collective-permute-start(bf16[16,128,128]{2,1,0:T(8,128)(2,1)S(1)} %collective-permute-done.23.mine_ref), channel_id=1, source_target_pairs={{0,8},{24,16},{1,9},{25,17},{2,10},{26,18},{3,11},{27,19},{4,12},{... | collective-permute-start | bytes 1572872 | tf_op jit(solution)/shard_map/ppermute | solution.py:550
  121.9 22.4 %collective-permute-start.19 = (bf16[16,128,128]{2,1,0:T(8,128)(2,1)}, bf16[16,128,128]{2,1,0:T(8,128)(2,1)S(1)}, u32[]{:S(2)}, u32[]{:S(2)}) collective-permute-start(bf16[16,128,128]{2,1,0:T(8,128)(2,1)} %copy-done.5), channel_id=1, source_target_pairs={{0,6},{1,7},{2,4},{3,5},{4,2},{5,3},{6,0},{7,1},{8,14},{9,15},{10,... | collective-permute-start | bytes 1572872 | tf_op jit(solution)/shard_map/ppermute | solution.py:563
  122.0 15.4 %collective-permute-start.21 = (bf16[8,128,128]{2,1,0:T(8,128)(2,1)S(1)}, bf16[8,128,128]{2,1,0:T(8,128)(2,1)S(1)}, u32[]{:S(2)}, u32[]{:S(2)}) collective-permute-start(bf16[8,128,128]{2,1,0:T(8,128)(2,1)S(1)} %slice.51.mine_ref), channel_id=1, source_target_pairs={{0,8},{24,16},{1,9},{25,17},{2,10},{26,18},{3,11},{27,19},{4,12},{... | collective-permute-start | bytes 786440 | tf_op jit(solution)/shard_map/ppermute | solution.py:526
  123.3 18.6 %collective-permute-start.25 = (bf16[8,128,128]{2,1,0:T(8,128)(2,1)S(1)}, bf16[8,128,128]{2,1,0:T(8,128)(2,1)S(1)}, u32[]{:S(2)}, u32[]{:S(2)}) collective-permute-start(bf16[8,128,128]{2,1,0:T(8,128)(2,1)S(1)} %merge.10.refs_4_.after_ref.mine_ref), channel_id=1, source_target_pairs={{8,16},{16,8},{9,17},{17,9},{10,18},{18,10},{11,19},{19,11},{12,20... | collective-permute-start | bytes 786440 | tf_op jit(solution)/shard_map/ppermute | solution.py:546
  137.5 23.3 %collective-permute-start.30 = (bf16[16,128,128]{2,1,0:T(8,128)(2,1)S(1)}, bf16[16,128,128]{2,1,0:T(8,128)(2,1)S(1)}, u32[]{:S(2)}, u32[]{:S(2)}) collective-permute-start(bf16[16,128,128]{2,1,0:T(8,128)(2,1)S(1)} %collective-permute-done.29.mine_ref), channel_id=1, source_target_pairs={{0,8},{24,16},{1,9},{25,17},{2,10},{26,18},{3,11},{27,19},{4,12},{... | collective-permute-start | bytes 1572872 | tf_op jit(solution)/shard_map/ppermute | solution.py:550
  142.1 19.5 %collective-permute-start.28 = (bf16[16,128,128]{2,1,0:T(8,128)(2,1)S(1)}, bf16[16,128,128]{2,1,0:T(8,128)(2,1)}, u32[]{:S(2)}, u32[]{:S(2)}) collective-permute-start(bf16[16,128,128]{2,1,0:T(8,128)(2,1)S(1)} %merge.13.after_ref.mine_ref), channel_id=1, source_target_pairs={{8,16},{16,8},{9,17},{17,9},{10,18},{18,10},{11,19},{19,11},{12,20... | collective-permute-start | bytes 1572872 | tf_op jit(solution)/shard_map/ppermute | solution.py:546
  143.6 7.0 %collective-permute-start.22 = (bf16[8,128,128]{2,1,0:T(8,128)(2,1)S(1)}, bf16[8,128,128]{2,1,0:T(8,128)(2,1)S(1)}, u32[]{:S(2)}, u32[]{:S(2)}) collective-permute-start(bf16[8,128,128]{2,1,0:T(8,128)(2,1)S(1)} %merge.11.after_ref.mine_ref), channel_id=1, source_target_pairs={{8,16},{16,8},{9,17},{17,9},{10,18},{18,10},{11,19},{19,11},{12,20... | collective-permute-start | bytes 786440 | tf_op jit(solution)/shard_map/ppermute | solution.py:546
  144.3 24.5 %collective-permute-start.20 = (bf16[16,128,128]{2,1,0:T(8,128)(2,1)S(1)}, bf16[16,128,128]{2,1,0:T(8,128)(2,1)S(1)}, u32[]{:S(2)}, u32[]{:S(2)}) collective-permute-start(bf16[16,128,128]{2,1,0:T(8,128)(2,1)S(1)} %collective-permute-done.19.mine_ref), channel_id=1, source_target_pairs={{0,8},{24,16},{1,9},{25,17},{2,10},{26,18},{3,11},{27,19},{4,12},{... | collective-permute-start | bytes 1572872 | tf_op jit(solution)/shard_map/ppermute | solution.py:550
  149.3 8.4 %collective-permute-start.27 = (bf16[8,128,128]{2,1,0:T(8,128)(2,1)S(1)}, bf16[8,128,128]{2,1,0:T(8,128)(2,1)}, u32[]{:S(2)}, u32[]{:S(2)}) collective-permute-start(bf16[8,128,128]{2,1,0:T(8,128)(2,1)S(1)} %merge.12.after_ref.refs_5_), channel_id=1, source_target_pairs={{8,0},{16,24},{9,1},{17,25},{10,2},{18,26},{11,3},{19,27},{12,4},{... | collective-permute-start | bytes 786440 | tf_op jit(solution)/shard_map/ppermute | solution.py:546
  150.7 15.5 %collective-permute-start.26 = (bf16[8,128,128]{2,1,0:T(8,128)(2,1)S(1)}, bf16[8,128,128]{2,1,0:T(8,128)(2,1)S(1)}, u32[]{:S(2)}, u32[]{:S(2)}) collective-permute-start(bf16[8,128,128]{2,1,0:T(8,128)(2,1)S(1)} %merge.14.refs_7_.refs_5_), channel_id=1, source_target_pairs={{8,0},{16,24},{9,1},{17,25},{10,2},{18,26},{11,3},{19,27},{12,4},{... | collective-permute-start | bytes 786440 | tf_op jit(solution)/shard_map/ppermute | solution.py:546
  160.9 8.8 %collective-permute-start.33 = (bf16[16,128,128]{2,1,0:T(8,128)(2,1)S(1)}, bf16[16,128,128]{2,1,0:T(8,128)(2,1)S(1)}, u32[]{:S(2)}, u32[]{:S(2)}) collective-permute-start(bf16[16,128,128]{2,1,0:T(8,128)(2,1)S(1)} %merge.15.after_ref.mine_ref), channel_id=1, source_target_pairs={{8,16},{16,8},{9,17},{17,9},{10,18},{18,10},{11,19},{19,11},{12,20... | collective-permute-start | bytes 1572872 | tf_op jit(solution)/shard_map/ppermute | solution.py:546
  162.7 18.6 %collective-permute-start.32 = (bf16[16,128,128]{2,1,0:T(8,128)(2,1)S(1)}, bf16[16,128,128]{2,1,0:T(8,128)(2,1)S(1)}, u32[]{:S(2)}, u32[]{:S(2)}) collective-permute-start(bf16[16,128,128]{2,1,0:T(8,128)(2,1)S(1)} %merge.16.refs_7_.refs_5_), channel_id=1, source_target_pairs={{8,0},{16,24},{9,1},{17,25},{10,2},{18,26},{11,3},{19,27},{12,4},{... | collective-permute-start | bytes 1572872 | tf_op jit(solution)/shard_map/ppermute | solution.py:546
  168.9 15.8 %collective-permute-start.31 = (bf16[16,128,128]{2,1,0:T(8,128)(2,1)S(1)}, bf16[16,128,128]{2,1,0:T(8,128)(2,1)S(1)}, u32[]{:S(2)}, u32[]{:S(2)}) collective-permute-start(bf16[16,128,128]{2,1,0:T(8,128)(2,1)S(1)} %merge.17.after_ref.mine_ref), channel_id=1, source_target_pairs={{8,16},{16,8},{9,17},{17,9},{10,18},{18,10},{11,19},{19,11},{12,20... | collective-permute-start | bytes 1572872 | tf_op jit(solution)/shard_map/ppermute | solution.py:546
  169.8 16.3 %copy-start.11 = (bf16[32,128,128]{2,1,0:T(8,128)(2,1)S(1)}, bf16[32,128,128]{2,1,0:T(8,128)(2,1)}, u32[]{:S(2)}) copy-start(bf16[32,128,128]{2,1,0:T(8,128)(2,1)} %get-tuple-element.36) | copy-start | bytes 3145732
  169.8 22.6 %collective-permute-start.35 = (bf16[16,128,128]{2,1,0:T(8,128)(2,1)S(1)}, bf16[16,128,128]{2,1,0:T(8,128)(2,1)S(1)}, u32[]{:S(2)}, u32[]{:S(2)}) collective-permute-start(bf16[16,128,128]{2,1,0:T(8,128)(2,1)S(1)} %merge.18.refs_7_.refs_5_), channel_id=1, source_target_pairs={{8,0},{16,24},{9,1},{17,25},{10,2},{18,26},{11,3},{19,27},{12,4},{... | collective-permute-start | bytes 1572872 | tf_op jit(solution)/shard_map/ppermute | solution.py:546
  184.8 16.4 %collective-permute-start.34 = (bf16[16,128,128]{2,1,0:T(8,128)(2,1)S(1)}, bf16[16,128,128]{2,1,0:T(8,128)(2,1)S(1)}, u32[]{:S(2)}, u32[]{:S(2)}) collective-permute-start(bf16[16,128,128]{2,1,0:T(8,128)(2,1)S(1)} %merge.19.refs_7_.refs_5_), channel_id=1, source_target_pairs={{8,0},{16,24},{9,1},{17,25},{10,2},{18,26},{11,3},{19,27},{12,4},{... | collective-permute-start | bytes 1572872 | tf_op jit(solution)/shard_map/ppermute | solution.py:546
